TPU v7x, 256 devices: a whole 4x4x8 slice. The times are simulated.
256 devices in a mesh: node: 32 (over z, x), feat: 8 (over y, core).
Axes of the slice: x: 4, y: 4, z: 8, core: 2. Of those that a mesh axis runs over, the one named last changes fastest.
Arguments:
- features: bfloat16 [262144, 256], P(('node', 'feat')), may hold values from -6 to 6
- weight: bfloat16 [256, 256], replicated, may hold values from -0.375 to 0.375
- adjacency: bfloat16 [16384, 128, 128], P('node'), may hold values from 0 to 0.076171875
- block_coords: int32 [2, 16384], P(None, 'node'), may hold values from 0 to 127, as said below
- block_counts: int32 [32], P('node'), may hold values from 128 to 512, as said below
- send_rows: int32 [1024, 256], P('node'), may hold values from 0 to 8191, as said below
- cotangent: bfloat16 [256, 262144], P('feat', 'node'), may hold values from -6 to 6
Outputs:
- activations: bfloat16 [256, 262144], P('feat', 'node')
- input_grad: bfloat16 [262144, 256], P(('node', 'feat'))
- weight_grad: float32 [256, 256], P(None, 'feat')
Inputs may be any that keep to these rules, and one draw needn't show every extreme that they name: `send_rows`: row q * 32 + p lists 256 distinct local rows (0 to 8191) of partition q sent to partition p. `block_coords`: per partition, slots 0 to 63 hold the diagonal blocks (r, r); slots 64 to 127 hold one block with column block 64 + h for each h; row blocks lie in 0 to 63, column blocks in 0 to 127; coordinates may repeat. `block_counts`: between 128 and 512; some partition has exactly 512.
All inputs are finite; a program needn't handle non-finite values.
Results may differ from a plain program's by a relative error of at most 0.0061.
Values may be sent and summed in bfloat16 or wider, within the bound.
A program may use at most 128 MiB of HBM per device.

v0:
```python
import math

import jax
import jax.numpy as jnp
from jax import lax
from jax.sharding import PartitionSpec as P


def aggregate(extended, block_rows, block_cols, blocks, count, row_blocks):
    max_blocks = blocks.shape[0]
    block_size = blocks.shape[1]
    width = extended.shape[0]
    active = jnp.arange(max_blocks, dtype=jnp.int32) < count
    tiles = extended.reshape(width, -1, block_size)
    picked = jnp.take(tiles, block_cols, axis=1)
    products = jnp.einsum("fbj,bij->fbi", picked, blocks, preferred_element_type=jnp.float32)
    row_hot = (
        (block_rows[:, None] == jnp.arange(row_blocks, dtype=jnp.int32)[None, :]) & active[:, None]
    ).astype(jnp.float32)
    summed = jnp.einsum("fbi,br->fri", products, row_hot, precision=lax.Precision.HIGHEST)
    return summed.reshape(width, row_blocks * block_size)


def spread_back(grad_pre, block_rows, block_cols, blocks, count, total_blocks):
    max_blocks = blocks.shape[0]
    block_size = blocks.shape[1]
    width = grad_pre.shape[0]
    active = (jnp.arange(max_blocks, dtype=jnp.int32) < count).astype(grad_pre.dtype)
    tiles = grad_pre.reshape(width, -1, block_size)
    picked = jnp.take(tiles, block_rows, axis=1) * active[None, :, None]
    contrib = jnp.einsum("fbi,bij->fbj", picked, blocks, preferred_element_type=jnp.float32)
    col_hot = (block_cols[:, None] == jnp.arange(total_blocks, dtype=jnp.int32)[None, :]).astype(
        jnp.float32
    )
    spread = jnp.einsum("fbj,bc->fcj", contrib, col_hot, precision=lax.Precision.HIGHEST)
    return spread.reshape(width, total_blocks * block_size)


def body(features, weight, adjacency, block_coords, block_counts, send_rows, cotangent):
    feat_count = lax.axis_size("feat")
    node_count = lax.axis_size("node")
    rows_dev, width = features.shape
    col_width = width // feat_count
    block_size = adjacency.shape[1]
    per_peer = send_rows.shape[1]
    part_rows = rows_dev * feat_count
    row_blocks = part_rows // block_size
    total_blocks = row_blocks + node_count * per_peer // block_size
    count = block_counts[0]
    block_rows = block_coords[0]
    block_cols = block_coords[1]
    projected_t = lax.dot_general(
        weight, features, (((0,), (1,)), ((), ())), preferred_element_type=jnp.float32
    ).astype(jnp.bfloat16)
    owned = lax.all_to_all(projected_t, "feat", split_axis=0, concat_axis=1, tiled=True)
    flat_rows = send_rows.reshape(-1)
    outgoing = jnp.take(owned, flat_rows, axis=1).reshape(col_width, node_count, per_peer)
    incoming = lax.all_to_all(outgoing, "node", split_axis=1, concat_axis=1, tiled=True).reshape(
        col_width, node_count * per_peer
    )
    extended = jnp.concatenate([owned, incoming], axis=1)
    preact = aggregate(extended, block_rows, block_cols, adjacency, count, row_blocks)
    sigma = jax.nn.sigmoid(preact)
    activations = (preact * sigma).astype(jnp.bfloat16)
    grad_pre = (cotangent.astype(jnp.float32) * sigma * (1.0 + preact * (1.0 - sigma))).astype(
        jnp.bfloat16
    )
    grad_ext = spread_back(grad_pre, block_rows, block_cols, adjacency, count, total_blocks)
    grad_local = grad_ext[:, :part_rows]
    grad_halo = grad_ext[:, part_rows:].reshape(col_width, node_count, per_peer)
    returned = lax.all_to_all(grad_halo, "node", split_axis=1, concat_axis=1, tiled=True).reshape(
        col_width, node_count * per_peer
    )
    grad_z = grad_local.at[:, flat_rows].add(returned).astype(jnp.bfloat16)
    scale = 1.0 / math.sqrt(node_count * part_rows)
    grad_piece = grad_z
    partial_grad = lax.dot_general(
        lax.all_gather(features, "feat", axis=0, tiled=True),
        grad_piece,
        (((0,), (1,)), ((), ())),
        preferred_element_type=jnp.float32,
    )
    weight_grad = lax.psum(partial_grad, "node") * scale
    weight_cols = lax.dynamic_slice_in_dim(weight, lax.axis_index("feat") * col_width, col_width, 1)
    grad_piece = grad_z
    input_grad = lax.psum_scatter(
        lax.dot_general(
            grad_piece, weight_cols, (((0,), (1,)), ((), ())), preferred_element_type=jnp.float32
        ),
        "feat",
        scatter_dimension=0,
        tiled=True,
    ).astype(jnp.bfloat16)
    return (activations, input_grad, weight_grad)


def solution(mesh):
    return jax.shard_map(
        body,
        mesh=mesh,
        in_specs=(
            P(("node", "feat"), None),
            P(),
            P("node", None, None),
            P(None, "node"),
            P("node"),
            P("node", None),
            P("feat", "node"),
        ),
        out_specs=(P("feat", "node"), P(("node", "feat"), None), P(None, "feat")),
        check_vma=False,
    )
```

profile of v0, /device:TPU:32, one launch (start us, length us, event | category | flops | bytes accessed | tf_op | source)
XLA Modules:
  0.0 374.7 jit_solution(14993021455849120458)
XLA Ops:
  7.2 0.0 copy-start
  7.2 0.0 all-gather.2.cloned.1.call-start
  7.2 0.7 all-gather.2.cloned.1.call-update
  7.9 0.2 copy-done
  8.1 2.2 convolution_convert_fusion
  10.3 4.5 %all-to-all-start = ((bf16[8,32,1024]{2,1,0:T(8,128)(2,1)}), bf16[8,32,1024]{2,1,0:T(8,128)(2,1)S(1)}, u32[]{:S(2)}, u32[]{:S(2)}) async-start(bf16[8,32,1024]{2,1,0:T(8,128)(2,1)} %bitcast.4), calls=%async_computation | async-start | bytes 1048576 | tf_op jit(solution)/shard_map/all_to_all | solution.py:55
  14.7 0.8 copy.55
  15.6 0.8 compare_and_fusion
  16.4 8.7 %all-to-all-done = bf16[8,32,1024]{2,1,0:T(8,128)(2,1)S(1)} async-done(((bf16[8,32,1024]{2,1,0:T(8,128)(2,1)}), bf16[8,32,1024]{2,1,0:T(8,128)(2,1)S(1)}, u32[]{:S(2)}, u32[]{:S(2)}) %all-to-all-start) | async-done | bytes 524320 | tf_op jit(solution)/shard_map/all_to_all | solution.py:55
  25.1 1.0 copy.39
  26.1 0.0 copy-start.2
  26.1 29.2 %gather_fusion = bf16[8192,32]{1,0:T(8,128)(2,1)} fusion(bf16[32,8192]{0,1:T(8,128)(2,1)S(1)} %bitcast.93, s32[8192]{0:T(1024)S(1)} %broadcast_clamp_fusion), kind=kCustom, calls=%fused_computation | custom fusion | bytes 1081344 | tf_op jit(solution)/shard_map/jit(_take)/gather | solution.py:57
  55.4 1.9 copy.40
  57.2 0.9 broadcast_select_fusion
  58.1 11.2 %all-to-all-start.1 = ((bf16[32,32,256]{2,0,1:T(8,128)(2,1)}), bf16[32,32,256]{2,0,1:T(8,128)(2,1)S(1)}, u32[]{:S(2)}, u32[]{:S(2)}) async-start(bf16[32,32,256]{2,0,1:T(8,128)(2,1)} %broadcast_select_fusion), calls=%async_computation.1 | async-start | bytes 1048576 | tf_op jit(solution)/shard_map/all_to_all | solution.py:58
  70.0 0.3 copy.38
  70.3 0.2 concatenate.8
  70.6 0.3 copy.42
  70.9 15.4 %all-to-all-done.1 = bf16[32,32,256]{2,0,1:T(8,128)(2,1)S(1)} async-done(((bf16[32,32,256]{2,0,1:T(8,128)(2,1)}), bf16[32,32,256]{2,0,1:T(8,128)(2,1)S(1)}, u32[]{:S(2)}, u32[]{:S(2)}) %all-to-all-start.1) | async-done | bytes 524320 | tf_op jit(solution)/shard_map/all_to_all | solution.py:58
  86.3 0.3 copy.41
  86.6 0.2 concatenate.9
  86.8 0.3 copy.43
  87.1 0.1 pad_maximum_fusion
  87.2 3.4 gather_fusion.1
  90.7 15.0 %fusion.13 = f32[32,512,128]{2,0,1:T(8,128)} fusion(bf16[512,128,128]{2,1,0:T(8,128)(2,1)} %param.9, bf16[512,32,128]{2,1,0:T(8,128)(2,1)} %gather_fusion.1, pred[512]{0:T(512)(128)(4,1)S(1)} %compare_and_fusion.2), kind=kOutput, calls=%fused_computation.17 | convolution fusion | flops 538968064 | bytes 29360640 | tf_op jit(solution)/shard_map/fbj,bij->fbi/dot_general | solution.py:16
  105.7 11.0 %fusion.2 = f32[64,32,128]{2,0,1:T(8,128)S(1)} fusion(f32[32,512,128]{2,0,1:T(8,128)} %fusion.13, s32[512]{0:T(512)S(1)} %bitcast.110, pred[512]{0:T(512)(128)(4,1)S(1)} %get-tuple-element.11), kind=kOutput, calls=%fused_computation.6 | convolution fusion | flops 1610678272 | bytes 9439744 | tf_op jit(solution)/shard_map/fbi,br->fri/dot_general | solution.py:20
  116.7 1.7 fusion.32
  118.4 0.1 copy.71
  118.5 3.5 gather_fusion.2
  121.9 9.6 %fusion.16 = f32[32,512,128]{2,0,1:T(8,128)S(1)} fusion(bf16[512,128,128]{2,1,0:T(8,128)(2,1)} %param.9, bf16[512,32,128]{2,1,0:T(8,128)(2,1)} %gather_fusion.2, pred[512]{0:T(512)(128)(4,1)S(1)} %compare_and_fusion.1, bf16[512]{0:T(512)(128)(2,1)S(1)} %get-tuple-element.12), kind=kOutput, calls=%fused_computation.18 | convolution fusion | flops 541065216 | bytes 29361664 | tf_op jit(solution)/shard_map/fbi,bij->fbj/dot_general | solution.py:31
  131.6 8.1 %fusion = f32[128,32,128]{2,0,1:T(8,128)S(1)} fusion(f32[32,512,128]{2,0,1:T(8,128)S(1)} %fusion.16, s32[512]{0:T(512)S(1)} %bitcast.108), kind=kOutput, calls=%fused_computation.4 | convolution fusion | flops 3221291008 | bytes 10487808 | tf_op jit(solution)/shard_map/fbj,bc->fcj/dot_general | solution.py:35
  139.6 1.2 copy.69
  140.8 0.1 fusion.46
  141.0 1.1 copy.70
  142.1 5.2 %all-to-all-start.2 = ((f32[32,32,256]{2,0,1:T(8,128)}), f32[32,32,256]{2,0,1:T(8,128)S(1)}, u32[]{:S(2)}, u32[]{:S(2)}) async-start(f32[32,32,256]{2,0,1:T(8,128)} %bitcast.89), calls=%async_computation.2 | async-start | bytes 2097152 | tf_op jit(solution)/shard_map/all_to_all | solution.py:71
  147.3 0.0 reduce-scatter.2.cloned.1.call-start
  147.3 2.9 copy.51
  150.2 23.6 %all-to-all-done.2 = f32[32,32,256]{2,0,1:T(8,128)S(1)} async-done(((f32[32,32,256]{2,0,1:T(8,128)}), f32[32,32,256]{2,0,1:T(8,128)S(1)}, u32[]{:S(2)}, u32[]{:S(2)}) %all-to-all-start.2) | async-done | bytes 1048608 | tf_op jit(solution)/shard_map/all_to_all | solution.py:71
  173.8 0.1 copy.54
  173.9 2.7 copy.50
  176.5 43.9 %scatter_fusion = f32[32,8192]{0,1:T(8,128)} fusion(f32[32,8192]{0,1:T(8,128)} %copy.51, s32[8192]{0:T(1024)S(1)} %bitcast.104, f32[8192,32]{1,0:T(8,128)} %copy.50), kind=kCustom, calls=%fused_computation.3 | custom fusion | flops 262144 | bytes 3178496 | tf_op jit(solution)/shard_map/scatter-add | solution.py:74
  220.5 6.7 %fusion.30 = f32[8192,256]{1,0:T(8,128)} fusion(f32[32,8192]{0,1:T(8,128)} %scatter_fusion, bf16[256,256]{1,0:T(8,128)(2,1)S(1)} %copy-done, s32[]{:T(128)S(6)} %select_n.74), kind=kOutput, calls=%fused_computation.38 | convolution fusion | flops 134479872 | bytes 9502724 | tf_op jit(solution)/shard_map/dot_general | solution.py:87
  227.2 0.0 reduce-scatter.2.cloned.1.call-update
  227.2 0.0 all-gather.2.cloned.1.call-done
  227.3 4.2 %convolution_bitcast_fusion = f32[256,32]{0,1:T(8,128)S(1)} fusion(bf16[8192,256]{1,0:T(8,128)(2,1)} %all-gather.2.cloned.1.call-done, f32[32,8192]{0,1:T(8,128)} %scatter_fusion), kind=kOutput, calls=%fused_computation.24 | convolution fusion | flops 134479872 | bytes 5275648 | tf_op jit(solution)/shard_map/dot_general | solution.py:77
  231.4 133.7 %psum.7 = f32[256,32]{0,1:T(8,128)S(1)} all-reduce(f32[256,32]{0,1:T(8,128)S(1)} %convolution_bitcast_fusion), channel_id=1, replica_groups=mesh['node'=32,'feat'=8] {'node'}, use_global_device_ids=true, to_apply=%region_2.3 | all-reduce | flops 8192 | bytes 65536 | tf_op jit(solution)/shard_map/psum | solution.py:83
  365.1 0.6 broadcast_multiply_fusion
  365.8 2.1 convert_element_type.33
  (13 shorter events, 0.1 us)
Async XLA Ops:
  7.2 0.9 copy-start
  7.2 220.1 %all-gather.2.cloned.1.call-start = ((), (), s32[]{:S(2)}) async-start(), calls=%async_computation.5 | async-start | bytes 4718592 | tf_op jit(solution)/shard_map/all_gather | solution.py:78
  10.3 14.8 %all-to-all-start = ((bf16[8,32,1024]{2,1,0:T(8,128)(2,1)}), bf16[8,32,1024]{2,1,0:T(8,128)(2,1)S(1)}, u32[]{:S(2)}, u32[]{:S(2)}) async-start(bf16[8,32,1024]{2,1,0:T(8,128)(2,1)} %bitcast.4), calls=%async_computation | async-start | bytes 1048576 | tf_op jit(solution)/shard_map/all_to_all | solution.py:55
  26.1 43.2 %copy-start.2 = (s32[2,512]{1,0:T(2,128)S(1)}, s32[2,512]{1,0:T(2,128)}, u32[]{:S(2)}) copy-start(s32[2,512]{1,0:T(2,128)} %param.10) | copy-start | bytes 12292
  58.1 28.2 %all-to-all-start.1 = ((bf16[32,32,256]{2,0,1:T(8,128)(2,1)}), bf16[32,32,256]{2,0,1:T(8,128)(2,1)S(1)}, u32[]{:S(2)}, u32[]{:S(2)}) async-start(bf16[32,32,256]{2,0,1:T(8,128)(2,1)} %broadcast_select_fusion), calls=%async_computation.1 | async-start | bytes 1048576 | tf_op jit(solution)/shard_map/all_to_all | solution.py:58
  105.7 11.0 %copy-start.1 = (bf16[32,8192]{1,0:T(8,128)(2,1)S(1)}, bf16[32,8192]{1,0:T(8,128)(2,1)}, u32[]{:S(2)}) copy-start(bf16[32,8192]{1,0:T(8,128)(2,1)} %param.13) | copy-start | bytes 1572868
  142.1 31.7 %all-to-all-start.2 = ((f32[32,32,256]{2,0,1:T(8,128)}), f32[32,32,256]{2,0,1:T(8,128)S(1)}, u32[]{:S(2)}, u32[]{:S(2)}) async-start(f32[32,32,256]{2,0,1:T(8,128)} %bitcast.89), calls=%async_computation.2 | async-start | bytes 2097152 | tf_op jit(solution)/shard_map/all_to_all | solution.py:71
  147.3 218.5 %reduce-scatter.2.cloned.1.call-start = ((), (), s32[]{:S(2)}) async-start(), calls=%async_computation.4 | async-start | bytes 9437184 | tf_op jit(solution)/shard_map/reduce_scatter | solution.py:86
Sparse Core Ops, SparseCore 0:
  9.9 37.2 all-gather.1
  227.4 50.5 reduce-scatter.1
where the time goes:
time: 381 us; the launch traced here: 375 us
  blocking collectives  134 us (35%)
  matrix products  56.8 us (15%)
  other arithmetic  50.1 us (13%)
  local copies, waits for them, and re-layouts  49.8 us (13%)
  waiting for transfers between devices  48.4 us (13%)
  starting transfers between devices  20.9 us (5%)
  between operations  14.9 us (4%)
    psum x1, blocking collectives, body(): weight_grad = lax.psum(partial_grad, 'node') * scale  134 us
    scatter-add x1, other arithmetic, body(): grad_z = grad_local.at[:, flat_rows].add(returned).astype(jnp.bfloat16)  43.9 us
    gather x2, local copies, waits for them, and re-layouts, body(): jnp.take(owned, flat_rows, axis=1).reshape(col_width, node_count, per_peer)  31.1 us
    all_to_all x1, waiting for transfers between devices, body(): lax.all_to_all(grad_halo, 'node', split_axis=1, concat_axis=1, tiled=True)  23.6 us
    all_to_all x1, waiting for transfers between devices, body(): lax.all_to_all(outgoing, 'node', split_axis=1, concat_axis=1, tiled=True)  15.4 us
    dot_general x1, matrix products, aggregate(): jnp.einsum('fbj,bij->fbi', picked, blocks, preferred_element_type=jnp.flo...  15 us
    all_to_all x1, starting transfers between devices, body(): lax.all_to_all(outgoing, 'node', split_axis=1, concat_axis=1, tiled=True)  11.2 us
    dot_general x1, matrix products, aggregate(): jnp.einsum('fbi,br->fri', products, row_hot, precision=lax.Precision.HIGH...  11 us
  transfers between devices with their start and end apart: 5, of which 3 were waited for; matrix products, arithmetic and copies ran while one was open for 41% of the time, Pallas kernels for 0%

commit v1 on v0

v1 whole, which is shorter than its diff:
```python
import functools
import math

import jax
import jax.numpy as jnp
from jax import lax
from jax.experimental import pallas as pl
from jax.experimental.pallas import tpu as pltpu
from jax.sharding import PartitionSpec as P

ZS, XS = 8, 4
NN = ZS * XS
NF = 8
F = 256
CW = F // NF
RD = 1024
LO = 256
GD = RD // LO
GP = NF * GD
HP = 256
BLK = 128
ROWB = 64
COLB = 128
MAXB = 512
MESH = pl.DeviceIdType.MESH
VMEM = pltpu.VMEM


def node_at(n, k):
    z = lax.rem(lax.div(n, XS) + lax.div(k, XS), ZS)
    x = lax.rem(lax.rem(n, XS) + lax.rem(k, XS), XS)
    return z * XS + x


def node_back(n, k):
    z = lax.rem(lax.div(n, XS) + ZS - lax.div(k, XS), ZS)
    x = lax.rem(lax.rem(n, XS) + XS - lax.rem(k, XS), XS)
    return z * XS + x


def enter(n, f):
    barrier = pltpu.get_barrier_semaphore()

    def greet_node(k, c):
        pl.semaphore_signal(barrier, inc=1, device_id={"node": node_at(n, k)}, device_id_type=MESH)
        return c

    def greet_feat(k, c):
        pl.semaphore_signal(barrier, inc=1, device_id={"feat": lax.rem(f + k, NF)}, device_id_type=MESH)
        return c

    lax.fori_loop(1, NF, greet_feat, 0)
    lax.fori_loop(1, NN, greet_node, 0)
    return barrier


def one_hot_t(lists, p):
    idx = lists[pl.ds(p, 1), :]
    lo = idx & (LO - 1)
    hi = lax.shift_right_logical(idx, 8)
    rows = lax.broadcasted_iota(jnp.int32, (LO, HP), 0)
    return (rows == lo).astype(jnp.float32).astype(jnp.bfloat16), hi


def forward_kernel(
    x_ref, w_ref, lists, own, halo, proj, packed, fsend, frecv, nsend, nrecv
):
    n = lax.axis_index("node")
    f = lax.axis_index("feat")
    barrier = enter(n, f)
    wt = w_ref[...].astype(jnp.float32).T.astype(jnp.bfloat16)
    for h in range(GD):
        proj[h] = lax.dot_general(
            wt,
            x_ref[h * LO : (h + 1) * LO, :],
            (((1,), (1,)), ((), ())),
            preferred_element_type=jnp.float32,
        ).astype(jnp.bfloat16)
    pl.semaphore_wait(barrier, NN + NF - 2)

    def feat_copy(k, to, source):
        return pltpu.make_async_remote_copy(
            src_ref=proj.at[:, pl.ds(pl.multiple_of(to * CW, CW), CW), :],
            dst_ref=own.at[pl.ds(source * GD, GD)],
            send_sem=fsend.at[k],
            recv_sem=frecv.at[k],
            device_id={"feat": to},
            device_id_type=MESH,
        )

    def start_feat(k, c):
        feat_copy(k, lax.rem(f + k, NF), f).start()
        return c

    lax.fori_loop(1, NF, start_feat, 0)
    own[pl.ds(f * GD, GD)] = proj[:, pl.ds(pl.multiple_of(f * CW, CW), CW), :]

    def wait_feat(k, c):
        feat_copy(k, lax.rem(f + k, NF), lax.rem(f + NF - k, NF)).wait_recv()
        return c

    lax.fori_loop(1, NF, wait_feat, 0)

    def pick(p):
        hot, hi = one_hot_t(lists, p)
        got = jnp.zeros((CW, HP), jnp.float32)
        step = 8
        for g in range(0, GP, step):
            part = jnp.dot(
                own[g : g + step].reshape(step * CW, LO), hot, preferred_element_type=jnp.float32
            )
            for h in range(step):
                got = jnp.where(hi == g + h, part[h * CW : (h + 1) * CW], got)
        return got.astype(jnp.bfloat16)

    def node_copy(k, to, source):
        return pltpu.make_async_remote_copy(
            src_ref=packed.at[k],
            dst_ref=halo.at[source],
            send_sem=nsend.at[k],
            recv_sem=nrecv.at[k],
            device_id={"node": to},
            device_id_type=MESH,
        )

    def send_node(i, c):
        k = NN - i
        to = node_at(n, k)
        packed[k] = pick(to)
        node_copy(k, to, n).start()
        return c

    lax.fori_loop(1, NN, send_node, 0)
    halo[n] = pick(n)

    def finish_node(i, c):
        k = NN - i
        node_copy(k, node_at(n, k), node_back(n, k)).wait()
        return c

    lax.fori_loop(1, NN, finish_node, 0)

    def finish_feat(k, c):
        feat_copy(k, lax.rem(f + k, NF), f).wait_send()
        return c

    lax.fori_loop(1, NF, finish_feat, 0)


def forward(features, weight, lists):
    part = jax.ShapeDtypeStruct((GP, CW, LO), jnp.bfloat16)
    return pl.pallas_call(
        forward_kernel,
        out_shape=(part, part),
        in_specs=[pl.BlockSpec(memory_space=VMEM)] * 3,
        out_specs=(pl.BlockSpec(memory_space=VMEM),) * 2,
        scratch_shapes=[
            VMEM((GD, F, LO), jnp.bfloat16),
            VMEM((NN, CW, HP), jnp.bfloat16),
            pltpu.SemaphoreType.DMA((NF,)),
            pltpu.SemaphoreType.DMA((NF,)),
            pltpu.SemaphoreType.DMA((NN,)),
            pltpu.SemaphoreType.DMA((NN,)),
        ],
        compiler_params=pltpu.CompilerParams(
            collective_id=0, has_side_effects=True, vmem_limit_bytes=32 * 2**20
        ),
        name="project_and_send",
    )(features, weight, lists)


CHUNKS = 16
PER_CHUNK = MAXB // CHUNKS
UNROLL = 8


def blocks_kernel(
    coords, counts, adj, own, halo, cot, act, local, remote, held, ext, pre, gpre, grad, sems
):
    def chunk(i):
        rows = pl.ds(i * PER_CHUNK, PER_CHUNK)
        return pltpu.make_async_copy(adj.at[rows], held.at[rows], sems.at[i])

    for i in range(CHUNKS):
        chunk(i).start()
    count = counts[0]
    pre[...] = jnp.zeros_like(pre)
    for g in range(GP):
        for s in range(2):
            ext[2 * g + s] = own[g, :, s * BLK : (s + 1) * BLK]
            ext[ROWB + 2 * g + s] = halo[g, :, s * BLK : (s + 1) * BLK]

    def row_of(b):
        return jnp.where(b < count, coords[0, b], ROWB)

    def gather_chunk(i, c):
        chunk(i).wait()

        def some(j, c):
            base = i * PER_CHUNK + j * UNROLL
            terms = []
            for u in range(UNROLL):
                b = base + u
                terms.append(
                    lax.dot_general(
                        ext[coords[1, b]],
                        held[b],
                        (((1,), (1,)), ((), ())),
                        preferred_element_type=jnp.float32,
                    )
                )
            for u in range(UNROLL):
                r = row_of(base + u)
                pre[r] = pre[r] + terms[u]
            return c

        return lax.fori_loop(0, PER_CHUNK // UNROLL, some, c)

    lax.fori_loop(0, CHUNKS, gather_chunk, 0)

    for r in range(ROWB):
        v = pre[r]
        at = slice(r * BLK, (r + 1) * BLK)
        sigma = jax.nn.sigmoid(v)
        act[:, at] = (v * sigma).astype(jnp.bfloat16)
        gpre[r] = (cot[:, at].astype(jnp.float32) * sigma * (1.0 + v * (1.0 - sigma))).astype(
            jnp.bfloat16
        )
    gpre[ROWB] = jnp.zeros((CW, BLK), jnp.bfloat16)
    grad[...] = jnp.zeros_like(grad)

    def spread(j, c):
        base = j * UNROLL
        terms = []
        for u in range(UNROLL):
            b = base + u
            terms.append(jnp.dot(gpre[row_of(b)], held[b], preferred_element_type=jnp.float32))
        for u in range(UNROLL):
            col = coords[1, base + u]
            grad[col] = grad[col] + terms[u]
        return c

    lax.fori_loop(0, MAXB // UNROLL, spread, 0)
    for g in range(GP):
        for s in range(2):
            at = slice(s * BLK, (s + 1) * BLK)
            local[g, :, at] = grad[2 * g + s]
            remote[g, :, at] = grad[ROWB + 2 * g + s].astype(jnp.bfloat16)


def blocks(coords, counts, adjacency, own, halo, cotangent):
    return pl.pallas_call(
        blocks_kernel,
        out_shape=(
            jax.ShapeDtypeStruct((CW, ROWB * BLK), jnp.bfloat16),
            jax.ShapeDtypeStruct((GP, CW, LO), jnp.float32),
            jax.ShapeDtypeStruct((NN, CW, HP), jnp.bfloat16),
        ),
        in_specs=[
            pl.BlockSpec(memory_space=pltpu.SMEM),
            pl.BlockSpec(memory_space=pltpu.SMEM),
            pl.BlockSpec(memory_space=pl.ANY),
            pl.BlockSpec(memory_space=VMEM),
            pl.BlockSpec(memory_space=VMEM),
            pl.BlockSpec(memory_space=VMEM),
        ],
        out_specs=(pl.BlockSpec(memory_space=VMEM),) * 3,
        scratch_shapes=[
            VMEM((MAXB, BLK, BLK), jnp.bfloat16),
            VMEM((COLB, CW, BLK), jnp.bfloat16),
            VMEM((ROWB + 1, CW, BLK), jnp.float32),
            VMEM((ROWB + 1, CW, BLK), jnp.bfloat16),
            VMEM((COLB, CW, BLK), jnp.float32),
            pltpu.SemaphoreType.DMA((CHUNKS,)),
        ],
        compiler_params=pltpu.CompilerParams(vmem_limit_bytes=40 * 2**20),
        name="blocks",
    )(coords, counts, adjacency, own, halo, cotangent)


def backward_kernel(
    remote, local, lists, x_ref, w_ref, in_grad, w_grad,
    landed, acc, gz, gz_rows, wpart, wland, pieces, pland, whole,
    nsend, nrecv, fsend, frecv, wsend, wrecv, psend, precv, asend, arecv,
):
    n = lax.axis_index("node")
    f = lax.axis_index("feat")
    barrier = enter(n, f)
    acc[...] = local[...]

    def add(p, vals):
        hot, hi = one_hot_t(lists, p)
        step = 8
        for g in range(0, GP, step):
            rows = jnp.concatenate(
                [jnp.where(hi == g + h, vals, 0.0).astype(jnp.bfloat16) for h in range(step)], axis=0
            )
            term = lax.dot_general(
                rows, hot, (((1,), (1,)), ((), ())), preferred_element_type=jnp.float32
            )
            acc[g : g + step] = acc[g : g + step] + term.reshape(step, CW, LO)

    pl.semaphore_wait(barrier, NN + NF - 2)

    def node_copy(k, to, source):
        return pltpu.make_async_remote_copy(
            src_ref=remote.at[to],
            dst_ref=landed.at[source],
            send_sem=nsend.at[k],
            recv_sem=nrecv.at[k],
            device_id={"node": to},
            device_id_type=MESH,
        )

    def start_node(k, c):
        node_copy(k, node_at(n, k), n).start()
        return c

    lax.fori_loop(1, NN, start_node, 0)
    add(n, remote[n].astype(jnp.float32))

    def take_node(k, c):
        source = node_back(n, k)
        node_copy(k, node_at(n, k), source).wait_recv()
        add(source, landed[source].astype(jnp.float32))
        return c

    lax.fori_loop(1, NN, take_node, 0)
    gz[...] = acc[...].astype(jnp.bfloat16)

    def feat_copy(k, to, source):
        return pltpu.make_async_remote_copy(
            src_ref=gz.at[pl.ds(to * GD, GD)],
            dst_ref=gz_rows.at[:, pl.ds(pl.multiple_of(source * CW, CW), CW), :],
            send_sem=fsend.at[k],
            recv_sem=frecv.at[k],
            device_id={"feat": to},
            device_id_type=MESH,
        )

    def start_feat(k, c):
        feat_copy(k, lax.rem(f + k, NF), f).start()
        return c

    lax.fori_loop(1, NF, start_feat, 0)
    gz_rows[:, pl.ds(pl.multiple_of(f * CW, CW), CW), :] = gz[pl.ds(f * GD, GD)]
    wt = w_ref[...].astype(jnp.float32).T.astype(jnp.bfloat16)

    def wait_feat(k, c):
        feat_copy(k, lax.rem(f + k, NF), lax.rem(f + NF - k, NF)).wait_recv()
        return c

    lax.fori_loop(1, NF, wait_feat, 0)

    total = jnp.zeros((F, F), jnp.float32)
    for h in range(GD):
        total = total + jnp.dot(
            gz_rows[h], x_ref[h * LO : (h + 1) * LO, :], preferred_element_type=jnp.float32
        )
    wpart[...] = total.reshape(NF, CW, F)

    def part_copy(k, to, source):
        return pltpu.make_async_remote_copy(
            src_ref=wpart.at[to],
            dst_ref=wland.at[source],
            send_sem=wsend.at[k],
            recv_sem=wrecv.at[k],
            device_id={"feat": to},
            device_id_type=MESH,
        )

    def start_part(k, c):
        part_copy(k, lax.rem(f + k, NF), f).start()
        return c

    lax.fori_loop(1, NF, start_part, 0)
    wland[f] = wpart[f]
    for h in range(GD):
        rows = gz_rows[h].astype(jnp.float32).T.astype(jnp.bfloat16)
        in_grad[h * LO : (h + 1) * LO, :] = jnp.dot(
            rows, wt, preferred_element_type=jnp.float32
        ).astype(jnp.bfloat16)

    def wait_part(k, c):
        part_copy(k, lax.rem(f + k, NF), lax.rem(f + NF - k, NF)).wait_recv()
        return c

    lax.fori_loop(1, NF, wait_part, 0)
    mine = wland[0]
    for g in range(1, NF):
        mine = mine + wland[g]
    mine = mine * (1.0 / math.sqrt(NN * ROWB * BLK))
    for i in range(CW):
        pieces[i] = mine[i : i + 1]

    def piece_copy(k, to, source):
        return pltpu.make_async_remote_copy(
            src_ref=pieces.at[to],
            dst_ref=pland.at[source],
            send_sem=psend.at[k],
            recv_sem=precv.at[k],
            device_id={"node": to},
            device_id_type=MESH,
        )

    def start_piece(k, c):
        piece_copy(k, node_at(n, k), n).start()
        return c

    lax.fori_loop(1, NN, start_piece, 0)
    pland[n] = pieces[n]

    def wait_piece(k, c):
        piece_copy(k, node_at(n, k), node_back(n, k)).wait_recv()
        return c

    lax.fori_loop(1, NN, wait_piece, 0)
    summed = pland[0]
    for i in range(1, NN):
        summed = summed + pland[i]
    whole[n] = summed

    def whole_copy(k, to, source):
        return pltpu.make_async_remote_copy(
            src_ref=whole.at[n],
            dst_ref=whole.at[source],
            send_sem=asend.at[k],
            recv_sem=arecv.at[k],
            device_id={"node": to},
            device_id_type=MESH,
        )

    def start_whole(k, c):
        whole_copy(k, node_at(n, k), n).start()
        return c

    lax.fori_loop(1, NN, start_whole, 0)

    def wait_whole(k, c):
        whole_copy(k, node_at(n, k), node_back(n, k)).wait_recv()
        return c

    lax.fori_loop(1, NN, wait_whole, 0)
    w_grad[...] = jnp.concatenate([whole[i] for i in range(CW)], axis=0).T

    def finish_node(k, c):
        node_copy(k, node_at(n, k), n).wait_send()
        piece_copy(k, node_at(n, k), n).wait_send()
        whole_copy(k, node_at(n, k), n).wait_send()
        return c

    lax.fori_loop(1, NN, finish_node, 0)

    def finish_feat(k, c):
        feat_copy(k, lax.rem(f + k, NF), f).wait_send()
        part_copy(k, lax.rem(f + k, NF), f).wait_send()
        return c

    lax.fori_loop(1, NF, finish_feat, 0)


def backward(remote, local, lists, features, weight):
    dma = pltpu.SemaphoreType.DMA
    return pl.pallas_call(
        backward_kernel,
        out_shape=(
            jax.ShapeDtypeStruct((RD, F), jnp.bfloat16),
            jax.ShapeDtypeStruct((F, CW), jnp.float32),
        ),
        in_specs=[pl.BlockSpec(memory_space=VMEM)] * 5,
        out_specs=(pl.BlockSpec(memory_space=VMEM),) * 2,
        scratch_shapes=[
            VMEM((NN, CW, HP), jnp.bfloat16),
            VMEM((GP, CW, LO), jnp.float32),
            VMEM((GP, CW, LO), jnp.bfloat16),
            VMEM((GD, F, LO), jnp.bfloat16),
            VMEM((NF, CW, F), jnp.float32),
            VMEM((NF, CW, F), jnp.float32),
            VMEM((NN, 1, F), jnp.float32),
            VMEM((NN, 1, F), jnp.float32),
            VMEM((NN, 1, F), jnp.float32),
            dma((NN,)),
            dma((NN,)),
            dma((NF,)),
            dma((NF,)),
            dma((NF,)),
            dma((NF,)),
            dma((NN,)),
            dma((NN,)),
            dma((NN,)),
            dma((NN,)),
        ],
        compiler_params=pltpu.CompilerParams(
            collective_id=1, has_side_effects=True, vmem_limit_bytes=32 * 2**20
        ),
        name="return_and_sum",
    )(remote, local, lists, features, weight)


def body(features, weight, adjacency, block_coords, block_counts, send_rows, cotangent):
    own, halo = forward(features, weight, send_rows)
    activations, local, remote = blocks(
        block_coords, block_counts, adjacency, own, halo, cotangent
    )
    input_grad, weight_grad = backward(remote, local, send_rows, features, weight)
    return (activations, input_grad, weight_grad)


def solution(mesh):
    return jax.shard_map(
        body,
        mesh=mesh,
        in_specs=(
            P(("node", "feat"), None),
            P(),
            P("node", None, None),
            P(None, "node"),
            P("node"),
            P("node", None),
            P("feat", "node"),
        ),
        out_specs=(P("feat", "node"), P(("node", "feat"), None), P(None, "feat")),
        check_vma=False,
    )
```

time: 381 us -> 129 us (0.34); the launches traced: 375 us -> 128 us
  blocking collectives: 134 us -> 0 us
  Pallas kernels: 0 us -> 121 us
  matrix products: 56.8 us -> 0 us
  other arithmetic: 50.1 us -> 0 us
  waiting for transfers between devices: 48.4 us -> 0 us
  local copies, waits for them, and re-layouts: 49.8 us -> 5.91 us
  starting transfers between devices: 20.9 us -> 0 us
  between operations: 14.9 us -> 1.35 us
    psum x1 -> x0, blocking collectives: 134 us -> none  [body(): weight_grad = lax.psum(partial_grad, 'node') * scale]
    pallas_call x0 -> x3, Pallas kernels: none -> 121 us  [the longest x1 52.4 us: backward(): pl.pallas_call(backward_kernel, out_shape=(jax.ShapeDtypeStruct((RD, F),...]
    dot_general x7 -> x0, matrix products: 56.8 us -> none  [the longest x1 15 us: aggregate(): jnp.einsum('fbj,bij->fbi', picked, blocks, preferred_element_type=jnp.flo...]
    all_to_all x3 -> x0, waiting for transfers between devices: 47.6 us -> none  [the longest x1 23.6 us: body(): lax.all_to_all(grad_halo, 'node', split_axis=1, concat_axis=1, tiled=True)]
    scatter-add x1 -> x0, other arithmetic: 43.9 us -> none  [body(): grad_z = grad_local.at[:, flat_rows].add(returned).astype(jnp.bfloat16)]
    gather x4 -> x0, local copies, waits for them, and re-layouts: 38 us -> none  [the longest x2 31.1 us: body(): jnp.take(owned, flat_rows, axis=1).reshape(col_width, node_count, per_peer)]
    all_to_all x3 -> x0, starting transfers between devices: 20.9 us -> none  [the longest x1 11.2 us: body(): lax.all_to_all(outgoing, 'node', split_axis=1, concat_axis=1, tiled=True)]
    reshape x4 -> x0, local copies, waits for them, and re-layouts: 3.93 us -> none  [the longest x2 2.75 us: body(): lax.all_to_all(grad_halo, 'node', split_axis=1, concat_axis=1, tiled=True)]
  transfers between devices with their start and end apart: 5 -> 0, of which waited for: 3 -> 0; matrix products, arithmetic and copies ran while one was open for 41% -> 0% of each run, Pallas kernels for 0% -> 0%
where the time goes in v1:
time: 129 us; the launch traced here: 128 us
  Pallas kernels  121 us (94%)
  local copies, waits for them, and re-layouts  5.91 us (5%)
  between operations  1.35 us (1%)
    pallas_call x1, Pallas kernels, backward(): pl.pallas_call(backward_kernel, out_shape=(jax.ShapeDtypeStruct((RD, F),...  52.4 us
    pallas_call x1, Pallas kernels, forward(): pl.pallas_call(forward_kernel, out_shape=(part, part), in_specs=[pl.Block...  36.4 us
    pallas_call x1, Pallas kernels, blocks(): pl.pallas_call(blocks_kernel, out_shape=(jax.ShapeDtypeStruct((CW, ROWB *...  31.7 us
    unnamed x18, local copies, waits for them, and re-layouts  5.91 us

profile of v1, /device:TPU:32, one launch (start us, length us, event | category | flops | bytes accessed | tf_op | source)
XLA Modules:
  0.0 127.8 jit_solution(13393328093791682015)
XLA Ops:
  1.3 0.0 copy-start
  1.3 1.0 copy-done
  2.3 0.0 copy-start.3
  2.3 0.9 copy-done.3
  3.2 0.0 copy-start.5
  3.2 0.8 copy-done.5
  4.0 0.0 copy-start.1
  4.0 0.0 copy-start.4
  4.0 0.0 copy-start.6
  4.0 36.4 %project_and_send.1 = (bf16[32,32,256]{2,1,0:T(8,128)(2,1)S(1)}, bf16[32,32,256]{2,1,0:T(8,128)(2,1)S(1)}) custom-call(bf16[1024,256]{1,0:T(8,128)(2,1)S(1)} %copy-done, bf16[256,256]{1,0:T(8,128)(2,1)S(1)} %copy-done.3, s32[32,256]{1,0:T(8,128)S(1)} %copy-done.5), custom_call_target="tpu_custom_call" | custom-call | tf_op jit(solution)/shard_map/project_and_send/pallas_call | solution.py:152
  40.4 0.0 copy-start.2
  40.5 1.0 copy-done.2
  41.5 0.0 copy-start.7
  41.5 0.7 copy-done.7
  42.2 31.7 %blocks.1 = (bf16[32,8192]{1,0:T(8,128)(2,1)}, f32[32,32,256]{2,1,0:T(8,128)S(1)}, bf16[32,32,256]{2,1,0:T(8,128)(2,1)S(1)}) custom-call(s32[2,512]{1,0:T(2,128)S(1)} %copy-done.7, s32[1]{0:T(128)S(6)} %copy.12.counts, bf16[512,128,128]{2,1,0:T(8,128)(2,1)} %adj.1, bf16[32,32,256]{2,1,0:T(8,128)(2,1)S(1)} %get-tuple-element.10.own, ...), custom_call_target="tpu_custom_call" | custom-call | tf_op jit(solution)/shard_map/blocks/pallas_call | solution.py:252
  73.9 0.0 copy-done.1
  73.9 0.0 copy-done.4
  73.9 0.0 copy-done.6
  73.9 52.4 %return_and_sum.1 = (bf16[1024,256]{1,0:T(8,128)(2,1)S(1)}, f32[256,32]{1,0:T(8,128)S(1)}) custom-call(bf16[32,32,256]{2,1,0:T(8,128)(2,1)S(1)} %get-tuple-element.13.remote, f32[32,32,256]{2,1,0:T(8,128)S(1)} %get-tuple-element.14.local, s32[32,256]{1,0:T(8,128)S(1)} %copy-done.6, bf16[1024,256]{1,0:T(8,128)(2,1)S(1)} %copy-done.1, ...), custom_call_target="tpu_custom_call" | custom-call | tf_op jit(solution)/shard_map/return_and_sum/pallas_call | solution.py:464
  126.3 0.7 copy.10
  127.0 0.8 copy.13
Async XLA Ops:
  1.3 1.0 copy-start
  2.3 0.9 copy-start.3
  3.2 0.8 copy-start.5
  4.0 69.9 %copy-start.1 = (bf16[1024,256]{1,0:T(8,128)(2,1)S(1)}, bf16[1024,256]{1,0:T(8,128)(2,1)}, u32[]{:S(2)}) copy-start(bf16[1024,256]{1,0:T(8,128)(2,1)} %x_ref.3) | copy-start | bytes 1572868
  4.0 69.9 %copy-start.4 = (bf16[256,256]{1,0:T(8,128)(2,1)S(1)}, bf16[256,256]{1,0:T(8,128)(2,1)}, u32[]{:S(2)}) copy-start(bf16[256,256]{1,0:T(8,128)(2,1)} %w_ref.3) | copy-start | bytes 393220
  4.0 69.9 %copy-start.6 = (s32[32,256]{1,0:T(8,128)S(1)}, s32[32,256]{1,0:T(8,128)}, u32[]{:S(2)}) copy-start(s32[32,256]{1,0:T(8,128)} %lists.3) | copy-start | bytes 98308
  40.4 1.0 copy-start.2
  41.5 0.7 copy-start.7

commit v2 on v1

--- a/solution.py
+++ b/solution.py
@@ -27,15 +27,23 @@
 
 
 def node_at(n, k):
-    z = lax.rem(lax.div(n, XS) + lax.div(k, XS), ZS)
-    x = lax.rem(lax.rem(n, XS) + lax.rem(k, XS), XS)
-    return z * XS + x
+    z = ((n & -XS) + (k & -XS)) & (NN - 1)
+    x = (n + k) & (XS - 1)
+    return z + x
 
 
 def node_back(n, k):
-    z = lax.rem(lax.div(n, XS) + ZS - lax.div(k, XS), ZS)
-    x = lax.rem(lax.rem(n, XS) + XS - lax.rem(k, XS), XS)
-    return z * XS + x
+    z = ((n & -XS) + NN - (k & -XS)) & (NN - 1)
+    x = (n + XS - (k & (XS - 1))) & (XS - 1)
+    return z + x
+
+
+def feat_at(f, k):
+    return (f + k) & (NF - 1)
+
+
+def feat_back(f, k):
+    return (f + NF - k) & (NF - 1)
 
 
 def enter(n, f):
@@ -46,7 +54,7 @@
         return c
 
     def greet_feat(k, c):
-        pl.semaphore_signal(barrier, inc=1, device_id={"feat": lax.rem(f + k, NF)}, device_id_type=MESH)
+        pl.semaphore_signal(barrier, inc=1, device_id={"feat": feat_at(f, k)}, device_id_type=MESH)
         return c
 
     lax.fori_loop(1, NF, greet_feat, 0)
@@ -63,11 +71,30 @@
 
 
 def forward_kernel(
-    x_ref, w_ref, lists, own, halo, proj, packed, fsend, frecv, nsend, nrecv
+    x_hbm, w_hbm, lists_hbm, adj_hbm, cot_hbm, coords_hbm,
+    own, halo, adj, cot, coords,
+    x_ref, w_ref, lists, proj, packed, fsend, frecv, nsend, nrecv, lsem,
 ):
     n = lax.axis_index("node")
     f = lax.axis_index("feat")
+    loads = [
+        pltpu.make_async_copy(src, dst, lsem.at[i])
+        for i, (src, dst) in enumerate(
+            [
+                (x_hbm, x_ref),
+                (w_hbm, w_ref),
+                (lists_hbm, lists),
+                (coords_hbm, coords),
+                (cot_hbm, cot),
+                (adj_hbm, adj),
+            ]
+        )
+    ]
+    for load in loads:
+        load.start()
     barrier = enter(n, f)
+    loads[0].wait()
+    loads[1].wait()
     wt = w_ref[...].astype(jnp.float32).T.astype(jnp.bfloat16)
     for h in range(GD):
         proj[h] = lax.dot_general(
@@ -89,14 +116,15 @@
         )
 
     def start_feat(k, c):
-        feat_copy(k, lax.rem(f + k, NF), f).start()
+        feat_copy(k, feat_at(f, k), f).start()
         return c
 
     lax.fori_loop(1, NF, start_feat, 0)
+    loads[2].wait()
     own[pl.ds(f * GD, GD)] = proj[:, pl.ds(pl.multiple_of(f * CW, CW), CW), :]
 
     def wait_feat(k, c):
-        feat_copy(k, lax.rem(f + k, NF), lax.rem(f + NF - k, NF)).wait_recv()
+        feat_copy(k, feat_at(f, k), feat_back(f, k)).wait_recv()
         return c
 
     lax.fori_loop(1, NF, wait_feat, 0)
@@ -141,82 +169,88 @@
     lax.fori_loop(1, NN, finish_node, 0)
 
     def finish_feat(k, c):
-        feat_copy(k, lax.rem(f + k, NF), f).wait_send()
+        feat_copy(k, feat_at(f, k), f).wait_send()
         return c
 
     lax.fori_loop(1, NF, finish_feat, 0)
-
-
-def forward(features, weight, lists):
+    for load in loads[3:]:
+        load.wait()
+
+
+def forward(features, weight, lists, adjacency, cotangent, coords):
     part = jax.ShapeDtypeStruct((GP, CW, LO), jnp.bfloat16)
+
+    def like(a):
+        return jax.ShapeDtypeStruct(a.shape, a.dtype)
+
     return pl.pallas_call(
         forward_kernel,
-        out_shape=(part, part),
-        in_specs=[pl.BlockSpec(memory_space=VMEM)] * 3,
-        out_specs=(pl.BlockSpec(memory_space=VMEM),) * 2,
+        out_shape=(part, part, like(adjacency), like(cotangent), like(coords)),
+        in_specs=[pl.BlockSpec(memory_space=pltpu.HBM)] * 6,
+        out_specs=(pl.BlockSpec(memory_space=VMEM),) * 5,
         scratch_shapes=[
+            VMEM((RD, F), jnp.bfloat16),
+            VMEM((F, F), jnp.bfloat16),
+            VMEM((NN, HP), jnp.int32),
             VMEM((GD, F, LO), jnp.bfloat16),
             VMEM((NN, CW, HP), jnp.bfloat16),
             pltpu.SemaphoreType.DMA((NF,)),
             pltpu.SemaphoreType.DMA((NF,)),
             pltpu.SemaphoreType.DMA((NN,)),
             pltpu.SemaphoreType.DMA((NN,)),
+            pltpu.SemaphoreType.DMA((6,)),
         ],
         compiler_params=pltpu.CompilerParams(
-            collective_id=0, has_side_effects=True, vmem_limit_bytes=32 * 2**20
+            collective_id=0, has_side_effects=True, vmem_limit_bytes=12 * 2**20
         ),
         name="project_and_send",
-    )(features, weight, lists)
-
-
-CHUNKS = 16
-PER_CHUNK = MAXB // CHUNKS
-UNROLL = 8
+    )(
+        *(
+            pltpu.with_memory_space_constraint(a, pltpu.HBM)
+            for a in (features, weight, lists, adjacency, cotangent, coords)
+        )
+    )
+
+
+UNROLL = 32
+NT = (((1,), (1,)), ((), ()))
 
 
 def blocks_kernel(
-    coords, counts, adj, own, halo, cot, act, local, remote, held, ext, pre, gpre, grad, sems
+    coords_v, counts, held, own, halo, cot, act, local, remote, coords, ext, pre, gpre, grad, sem
 ):
-    def chunk(i):
-        rows = pl.ds(i * PER_CHUNK, PER_CHUNK)
-        return pltpu.make_async_copy(adj.at[rows], held.at[rows], sems.at[i])
-
-    for i in range(CHUNKS):
-        chunk(i).start()
+    load = pltpu.make_async_copy(coords_v, coords, sem)
+    load.start()
     count = counts[0]
     pre[...] = jnp.zeros_like(pre)
+    grad[...] = jnp.zeros_like(grad)
     for g in range(GP):
         for s in range(2):
             ext[2 * g + s] = own[g, :, s * BLK : (s + 1) * BLK]
             ext[ROWB + 2 * g + s] = halo[g, :, s * BLK : (s + 1) * BLK]
+    load.wait()
 
     def row_of(b):
         return jnp.where(b < count, coords[0, b], ROWB)
 
-    def gather_chunk(i, c):
-        chunk(i).wait()
-
-        def some(j, c):
-            base = i * PER_CHUNK + j * UNROLL
-            terms = []
-            for u in range(UNROLL):
-                b = base + u
-                terms.append(
-                    lax.dot_general(
-                        ext[coords[1, b]],
-                        held[b],
-                        (((1,), (1,)), ((), ())),
-                        preferred_element_type=jnp.float32,
-                    )
-                )
-            for u in range(UNROLL):
-                r = row_of(base + u)
-                pre[r] = pre[r] + terms[u]
-            return c
-
-        return lax.fori_loop(0, PER_CHUNK // UNROLL, some, c)
-
-    lax.fori_loop(0, CHUNKS, gather_chunk, 0)
+    def gather(j, c):
+        base = j * UNROLL
+        terms = []
+        for b in [base + u for u in range(0, UNROLL, 2)]:
+            cols = jnp.concatenate([ext[coords[1, b]], ext[coords[1, b + 1]]], axis=0)
+            pair = lax.dot_general(
+                cols,
+                held[pl.ds(b, 2)].reshape(2 * BLK, BLK),
+                NT,
+                preferred_element_type=jnp.float32,
+            )
+            terms += [pair[:CW, :BLK], pair[CW:, BLK:]]
+        for u in range(UNROLL):
+            r = row_of(base + u)
+            pre[r] = pre[r] + terms[u]
+        return c
+
+    lax.fori_loop(0, MAXB // UNROLL, gather, 0)
 
     for r in range(ROWB):
         v = pre[r]
@@ -227,14 +261,18 @@
             jnp.bfloat16
         )
     gpre[ROWB] = jnp.zeros((CW, BLK), jnp.bfloat16)
-    grad[...] = jnp.zeros_like(grad)
 
     def spread(j, c):
         base = j * UNROLL
         terms = []
-        for u in range(UNROLL):
-            b = base + u
-            terms.append(jnp.dot(gpre[row_of(b)], held[b], preferred_element_type=jnp.float32))
+        for b in [base + u for u in range(0, UNROLL, 2)]:
+            rows = jnp.concatenate([gpre[row_of(b)], gpre[row_of(b + 1)]], axis=0)
+            pair = jnp.dot(
+                rows,
+                jnp.concatenate([held[b], held[b + 1]], axis=1),
+                preferred_element_type=jnp.float32,
+            )
+            terms += [pair[:CW, :BLK], pair[CW:, BLK:]]
         for u in range(UNROLL):
             col = coords[1, base + u]
             grad[col] = grad[col] + terms[u]
@@ -257,31 +295,31 @@
             jax.ShapeDtypeStruct((NN, CW, HP), jnp.bfloat16),
         ),
         in_specs=[
+            pl.BlockSpec(memory_space=VMEM),
             pl.BlockSpec(memory_space=pltpu.SMEM),
-            pl.BlockSpec(memory_space=pltpu.SMEM),
-            pl.BlockSpec(memory_space=pl.ANY),
+            pl.BlockSpec(memory_space=VMEM),
             pl.BlockSpec(memory_space=VMEM),
             pl.BlockSpec(memory_space=VMEM),
             pl.BlockSpec(memory_space=VMEM),
         ],
         out_specs=(pl.BlockSpec(memory_space=VMEM),) * 3,
         scratch_shapes=[
-            VMEM((MAXB, BLK, BLK), jnp.bfloat16),
+            pltpu.SMEM((2, MAXB), jnp.int32),
             VMEM((COLB, CW, BLK), jnp.bfloat16),
             VMEM((ROWB + 1, CW, BLK), jnp.float32),
             VMEM((ROWB + 1, CW, BLK), jnp.bfloat16),
             VMEM((COLB, CW, BLK), jnp.float32),
-            pltpu.SemaphoreType.DMA((CHUNKS,)),
+            pltpu.SemaphoreType.DMA,
         ],
-        compiler_params=pltpu.CompilerParams(vmem_limit_bytes=40 * 2**20),
+        compiler_params=pltpu.CompilerParams(vmem_limit_bytes=14 * 2**20),
         name="blocks",
     )(coords, counts, adjacency, own, halo, cotangent)
 
 
 def backward_kernel(
     remote, local, lists, x_ref, w_ref, in_grad, w_grad,
-    landed, acc, gz, gz_rows, wpart, wland, pieces, pland, whole,
-    nsend, nrecv, fsend, frecv, wsend, wrecv, psend, precv, asend, arecv,
+    landed, acc, gz, gz_rows, wpart, wland, pieces, pland, zpart, zland, whole,
+    nsend, nrecv, fsend, frecv, wsend, wrecv, psend, precv, zsend, zrecv, asend, arecv,
 ):
     n = lax.axis_index("node")
     f = lax.axis_index("feat")
@@ -339,7 +377,7 @@
         )
 
     def start_feat(k, c):
-        feat_copy(k, lax.rem(f + k, NF), f).start()
+        feat_copy(k, feat_at(f, k), f).start()
         return c
 
     lax.fori_loop(1, NF, start_feat, 0)
@@ -347,7 +385,7 @@
     wt = w_ref[...].astype(jnp.float32).T.astype(jnp.bfloat16)
 
     def wait_feat(k, c):
-        feat_copy(k, lax.rem(f + k, NF), lax.rem(f + NF - k, NF)).wait_recv()
+        feat_copy(k, feat_at(f, k), feat_back(f, k)).wait_recv()
         return c
 
     lax.fori_loop(1, NF, wait_feat, 0)
@@ -370,7 +408,7 @@
         )
 
     def start_part(k, c):
-        part_copy(k, lax.rem(f + k, NF), f).start()
+        part_copy(k, feat_at(f, k), f).start()
         return c
 
     lax.fori_loop(1, NF, start_part, 0)
@@ -382,7 +420,7 @@
         ).astype(jnp.bfloat16)
 
     def wait_part(k, c):
-        part_copy(k, lax.rem(f + k, NF), lax.rem(f + NF - k, NF)).wait_recv()
+        part_copy(k, feat_at(f, k), feat_back(f, k)).wait_recv()
         return c
 
     lax.fori_loop(1, NF, wait_part, 0)
@@ -390,70 +428,83 @@
     for g in range(1, NF):
         mine = mine + wland[g]
     mine = mine * (1.0 / math.sqrt(NN * ROWB * BLK))
-    for i in range(CW):
-        pieces[i] = mine[i : i + 1]
-
-    def piece_copy(k, to, source):
-        return pltpu.make_async_remote_copy(
-            src_ref=pieces.at[to],
-            dst_ref=pland.at[source],
+    z, x = n & -XS, n & (XS - 1)
+    pieces[...] = mine.reshape(XS, CW // XS, F)
+
+    def x_at(k):
+        return z + ((x + k) & (XS - 1))
+
+    def z_at(k):
+        return ((z + XS * k) & (NN - 1)) + x
+
+    def share_copy(k, source):
+        to = x_at(k)
+        return pltpu.make_async_remote_copy(
+            src_ref=pieces.at[to & (XS - 1)],
+            dst_ref=pland.at[source & (XS - 1)],
             send_sem=psend.at[k],
             recv_sem=precv.at[k],
             device_id={"node": to},
             device_id_type=MESH,
         )
 
-    def start_piece(k, c):
-        piece_copy(k, node_at(n, k), n).start()
-        return c
-
-    lax.fori_loop(1, NN, start_piece, 0)
-    pland[n] = pieces[n]
-
-    def wait_piece(k, c):
-        piece_copy(k, node_at(n, k), node_back(n, k)).wait_recv()
-        return c
-
-    lax.fori_loop(1, NN, wait_piece, 0)
-    summed = pland[0]
-    for i in range(1, NN):
-        summed = summed + pland[i]
-    whole[n] = summed
-
-    def whole_copy(k, to, source):
-        return pltpu.make_async_remote_copy(
-            src_ref=whole.at[n],
-            dst_ref=whole.at[source],
+    for k in range(1, XS):
+        share_copy(k, n).start()
+    pland[x] = pieces[x]
+    for k in range(1, XS):
+        share_copy(k, x_at(XS - k)).wait_recv()
+    zpart[...] = pland[0] + pland[1] + pland[2] + pland[3]
+
+    def z_copy(k, source):
+        return pltpu.make_async_remote_copy(
+            src_ref=zpart,
+            dst_ref=zland.at[lax.shift_right_logical(source, 2)],
+            send_sem=zsend.at[k],
+            recv_sem=zrecv.at[k],
+            device_id={"node": z_at(k)},
+            device_id_type=MESH,
+        )
+
+    for k in range(1, ZS):
+        z_copy(k, n).start()
+    zland[lax.shift_right_logical(n, 2)] = zpart[...]
+    for k in range(1, ZS):
+        z_copy(k, z_at(ZS - k)).wait_recv()
+    summed = zland[0]
+    for i in range(1, ZS):
+        summed = summed + zland[i]
+    whole[x] = summed
+
+    def back_copy(k, source):
+        return pltpu.make_async_remote_copy(
+            src_ref=whole.at[x],
+            dst_ref=whole.at[source & (XS - 1)],
             send_sem=asend.at[k],
             recv_sem=arecv.at[k],
-            device_id={"node": to},
-            device_id_type=MESH,
-        )
-
-    def start_whole(k, c):
-        whole_copy(k, node_at(n, k), n).start()
-        return c
-
-    lax.fori_loop(1, NN, start_whole, 0)
-
-    def wait_whole(k, c):
-        whole_copy(k, node_at(n, k), node_back(n, k)).wait_recv()
-        return c
-
-    lax.fori_loop(1, NN, wait_whole, 0)
-    w_grad[...] = jnp.concatenate([whole[i] for i in range(CW)], axis=0).T
+            device_id={"node": x_at(k)},
+            device_id_type=MESH,
+        )
+
+    for k in range(1, XS):
+        back_copy(k, n).start()
+    for k in range(1, XS):
+        back_copy(k, x_at(XS - k)).wait_recv()
+    w_grad[...] = whole[...].reshape(CW, F)
+    for k in range(1, XS):
+        share_copy(k, n).wait_send()
+        back_copy(k, n).wait_send()
+    for k in range(1, ZS):
+        z_copy(k, n).wait_send()
 
     def finish_node(k, c):
         node_copy(k, node_at(n, k), n).wait_send()
-        piece_copy(k, node_at(n, k), n).wait_send()
-        whole_copy(k, node_at(n, k), n).wait_send()
         return c
 
     lax.fori_loop(1, NN, finish_node, 0)
 
     def finish_feat(k, c):
-        feat_copy(k, lax.rem(f + k, NF), f).wait_send()
-        part_copy(k, lax.rem(f + k, NF), f).wait_send()
+        feat_copy(k, feat_at(f, k), f).wait_send()
+        part_copy(k, feat_at(f, k), f).wait_send()
         return c
 
     lax.fori_loop(1, NF, finish_feat, 0)
@@ -465,7 +516,7 @@
         backward_kernel,
         out_shape=(
             jax.ShapeDtypeStruct((RD, F), jnp.bfloat16),
-            jax.ShapeDtypeStruct((F, CW), jnp.float32),
+            jax.ShapeDtypeStruct((CW, F), jnp.float32),
         ),
         in_specs=[pl.BlockSpec(memory_space=VMEM)] * 5,
         out_specs=(pl.BlockSpec(memory_space=VMEM),) * 2,
@@ -476,19 +527,23 @@
             VMEM((GD, F, LO), jnp.bfloat16),
             VMEM((NF, CW, F), jnp.float32),
             VMEM((NF, CW, F), jnp.float32),
-            VMEM((NN, 1, F), jnp.float32),
-            VMEM((NN, 1, F), jnp.float32),
-            VMEM((NN, 1, F), jnp.float32),
+            VMEM((XS, CW // XS, F), jnp.float32),
+            VMEM((XS, CW // XS, F), jnp.float32),
+            VMEM((CW // XS, F), jnp.float32),
+            VMEM((ZS, CW // XS, F), jnp.float32),
+            VMEM((XS, CW // XS, F), jnp.float32),
             dma((NN,)),
             dma((NN,)),
             dma((NF,)),
             dma((NF,)),
             dma((NF,)),
             dma((NF,)),
-            dma((NN,)),
-            dma((NN,)),
-            dma((NN,)),
-            dma((NN,)),
+            dma((XS,)),
+            dma((XS,)),
+            dma((ZS,)),
+            dma((ZS,)),
+            dma((XS,)),
+            dma((XS,)),
         ],
         compiler_params=pltpu.CompilerParams(
             collective_id=1, has_side_effects=True, vmem_limit_bytes=32 * 2**20
@@ -498,11 +553,12 @@
 
 
 def body(features, weight, adjacency, block_coords, block_counts, send_rows, cotangent):
-    own, halo = forward(features, weight, send_rows)
-    activations, local, remote = blocks(
-        block_coords, block_counts, adjacency, own, halo, cotangent
+    own, halo, held, cot, coords = forward(
+        features, weight, send_rows, adjacency, cotangent, block_coords
     )
-    input_grad, weight_grad = backward(remote, local, send_rows, features, weight)
+    activations, local, remote = blocks(coords, block_counts, held, own, halo, cot)
+    input_grad, weight_grad_t = backward(remote, local, send_rows, features, weight)
+    weight_grad = weight_grad_t.T
     return (activations, input_grad, weight_grad)
 
 

time: 129 us -> 105 us (0.81)
  Pallas kernels: 121 us -> 101 us
  local copies, waits for them, and re-layouts: 5.91 us -> 1.42 us
    pallas_call x1, Pallas kernels: 31.7 us -> 15.4 us  [blocks(): pl.pallas_call(blocks_kernel, out_shape=(jax.ShapeDtypeStruct((CW, ROWB *...]
    unnamed x18 -> x8, local copies, waits for them, and re-layouts: 5.91 us -> 1.42 us
    pallas_call x1, Pallas kernels: 52.4 us -> 49.4 us  [backward(): pl.pallas_call(backward_kernel, out_shape=(jax.ShapeDtypeStruct((RD, F),...]
where the time goes in v2:
time: 105 us; the launch traced here: 104 us
  Pallas kernels  101 us (96%)
  local copies, waits for them, and re-layouts  1.42 us (1%)
  between operations  1.35 us (1%)
    pallas_call x1, Pallas kernels, backward(): pl.pallas_call(backward_kernel, out_shape=(jax.ShapeDtypeStruct((RD, F),...  49.4 us
    pallas_call x1, Pallas kernels, forward(): pl.pallas_call(forward_kernel, out_shape=(part, part, like(adjacency), li...  36.5 us
    pallas_call x1, Pallas kernels, blocks(): pl.pallas_call(blocks_kernel, out_shape=(jax.ShapeDtypeStruct((CW, ROWB *...  15.4 us

profile of v2, /device:TPU:32, one launch (start us, length us, event | category | flops | bytes accessed | tf_op | source)
XLA Modules:
  0.0 104.1 jit_solution(4339713617331872962)
XLA Ops:
  1.3 0.0 copy-start
  1.3 0.0 copy-start.1
  1.3 0.0 copy-start.2
  1.3 36.5 %project_and_send.1 = (bf16[32,32,256]{2,1,0:T(8,128)(2,1)S(1)}, bf16[32,32,256]{2,1,0:T(8,128)(2,1)S(1)}, bf16[512,128,128]{2,1,0:T(8,128)(2,1)S(1)}, bf16[32,8192]{1,0:T(8,128)(2,1)S(1)}, s32[2,512]{1,0:T(2,128)S(1)}) custom-call(bf16[1024,256]{1,0:T(8,128)(2,1)} %x_ref.1, bf16[256,256]{1,0:T(8,128)(2,1)} %w_ref.1, s32[32,256]{1,0:T(8,128)} %lists.1, ...), custom_call_target="tpu_custom_call" | custom-call | tf_op jit(solution)/shard_map/project_and_send/pallas_call | solution.py:186
  37.8 15.4 %blocks.1 = (bf16[32,8192]{1,0:T(8,128)(2,1)}, f32[32,32,256]{2,1,0:T(8,128)S(1)}, bf16[32,32,256]{2,1,0:T(8,128)(2,1)S(1)}) custom-call(s32[2,512]{1,0:T(2,128)S(1)} %get-tuple-element.13.coords_v, s32[1]{0:T(128)S(6)} %copy.12.counts, bf16[512,128,128]{2,1,0:T(8,128)(2,1)S(1)} %get-tuple-element.14.held, bf16[32,32,256]{2,1,0:T(8,128)(2,1)S(1)} %get-tuple-element.15.own, ...), custom_call_target="tpu_custom_call" | custom-call | tf_op jit(solution)/shard_map/blocks/pallas_call | solution.py:290
  53.3 0.0 copy-done
  53.3 0.0 copy-done.1
  53.3 0.0 copy-done.2
  53.3 49.4 %return_and_sum.1 = (bf16[1024,256]{1,0:T(8,128)(2,1)S(1)}, f32[32,256]{1,0:T(8,128)S(1)}) custom-call(bf16[32,32,256]{2,1,0:T(8,128)(2,1)S(1)} %get-tuple-element.19.remote, f32[32,32,256]{2,1,0:T(8,128)S(1)} %get-tuple-element.20.local, s32[32,256]{1,0:T(8,128)S(1)} %copy-done.2, bf16[1024,256]{1,0:T(8,128)(2,1)S(1)} %copy-done, bf16[256,256]{1,0:T(8,128)(2,1)S(1)} %copy-done.1), custom_call_target="tpu_custom_call" | custom-call | tf_op jit(solution)/shard_map/return_and_sum/pallas_call | solution.py:515
  102.7 0.8 copy.13
  103.5 0.6 copy.14
Async XLA Ops:
  1.3 52.0 %copy-start = (bf16[1024,256]{1,0:T(8,128)(2,1)S(1)}, bf16[1024,256]{1,0:T(8,128)(2,1)}, u32[]{:S(2)}) copy-start(bf16[1024,256]{1,0:T(8,128)(2,1)} %x_ref.1) | copy-start | bytes 1572868
  1.3 52.0 %copy-start.1 = (bf16[256,256]{1,0:T(8,128)(2,1)S(1)}, bf16[256,256]{1,0:T(8,128)(2,1)}, u32[]{:S(2)}) copy-start(bf16[256,256]{1,0:T(8,128)(2,1)} %w_ref.1) | copy-start | bytes 393220
  1.3 52.0 %copy-start.2 = (s32[32,256]{1,0:T(8,128)S(1)}, s32[32,256]{1,0:T(8,128)}, u32[]{:S(2)}) copy-start(s32[32,256]{1,0:T(8,128)} %lists.1) | copy-start | bytes 98308

commit v3 on v2

--- a/solution.py
+++ b/solution.py
@@ -11,6 +11,7 @@
 ZS, XS = 8, 4
 NN = ZS * XS
 NF = 8
+NY = 4
 F = 256
 CW = F // NF
 RD = 1024
@@ -72,11 +73,13 @@
 
 def forward_kernel(
     x_hbm, w_hbm, lists_hbm, adj_hbm, cot_hbm, coords_hbm,
-    own, halo, adj, cot, coords,
-    x_ref, w_ref, lists, proj, packed, fsend, frecv, nsend, nrecv, lsem,
+    own, halo, xs, adj, cot, coords,
+    w_ref, lists, proj, packed, fsend, frecv, nsend, nrecv, xsend, xrecv, lsem,
 ):
     n = lax.axis_index("node")
     f = lax.axis_index("feat")
+    y = lax.shift_right_logical(f, 1)
+    x_ref = xs.at[y]
     loads = [
         pltpu.make_async_copy(src, dst, lsem.at[i])
         for i, (src, dst) in enumerate(
@@ -99,7 +102,7 @@
     for h in range(GD):
         proj[h] = lax.dot_general(
             wt,
-            x_ref[h * LO : (h + 1) * LO, :],
+            xs[y, h * LO : (h + 1) * LO, :],
             (((1,), (1,)), ((), ())),
             preferred_element_type=jnp.float32,
         ).astype(jnp.bfloat16)
@@ -128,6 +131,19 @@
         return c
 
     lax.fori_loop(1, NF, wait_feat, 0)
+
+    def rows_copy(k, source):
+        return pltpu.make_async_remote_copy(
+            src_ref=xs.at[y],
+            dst_ref=xs.at[source],
+            send_sem=xsend.at[k],
+            recv_sem=xrecv.at[k],
+            device_id={"feat": feat_at(f, 2 * k)},
+            device_id_type=MESH,
+        )
+
+    for k in (1, 3):
+        rows_copy(k, y).start()
 
     def pick(p):
         hot, hi = one_hot_t(lists, p)
@@ -173,6 +189,8 @@
         return c
 
     lax.fori_loop(1, NF, finish_feat, 0)
+    for k in (1, 3):
+        rows_copy(k, (y + NY - k) & (NY - 1)).wait()
     for load in loads[3:]:
         load.wait()
 
@@ -185,11 +203,17 @@
 
     return pl.pallas_call(
         forward_kernel,
-        out_shape=(part, part, like(adjacency), like(cotangent), like(coords)),
+        out_shape=(
+            part,
+            part,
+            jax.ShapeDtypeStruct((NY, RD, F), jnp.bfloat16),
+            like(adjacency),
+            like(cotangent),
+            like(coords),
+        ),
         in_specs=[pl.BlockSpec(memory_space=pltpu.HBM)] * 6,
-        out_specs=(pl.BlockSpec(memory_space=VMEM),) * 5,
+        out_specs=(pl.BlockSpec(memory_space=VMEM),) * 6,
         scratch_shapes=[
-            VMEM((RD, F), jnp.bfloat16),
             VMEM((F, F), jnp.bfloat16),
             VMEM((NN, HP), jnp.int32),
             VMEM((GD, F, LO), jnp.bfloat16),
@@ -198,6 +222,8 @@
             pltpu.SemaphoreType.DMA((NF,)),
             pltpu.SemaphoreType.DMA((NN,)),
             pltpu.SemaphoreType.DMA((NN,)),
+            pltpu.SemaphoreType.DMA((NY,)),
+            pltpu.SemaphoreType.DMA((NY,)),
             pltpu.SemaphoreType.DMA((6,)),
         ],
         compiler_params=pltpu.CompilerParams(
@@ -317,12 +343,15 @@
 
 
 def backward_kernel(
-    remote, local, lists, x_ref, w_ref, in_grad, w_grad,
-    landed, acc, gz, gz_rows, wpart, wland, pieces, pland, zpart, zland, whole,
-    nsend, nrecv, fsend, frecv, wsend, wrecv, psend, precv, zsend, zrecv, asend, arecv,
+    remote, local, lists, xs, w_ref, in_grad, w_grad,
+    x_far, x_other, landed, acc, gz, gz_rows, pieces, pland, zpart, zland, whole,
+    nsend, nrecv, fsend, frecv, xsend, xrecv, osend, orecv, psend, precv, zsend, zrecv, asend, arecv,
 ):
     n = lax.axis_index("node")
     f = lax.axis_index("feat")
+    y = lax.shift_right_logical(f, 1)
+    core = f & 1
+    far = y ^ 2
     barrier = enter(n, f)
     acc[...] = local[...]
 
@@ -355,6 +384,28 @@
         return c
 
     lax.fori_loop(1, NN, start_node, 0)
+    far_copy = pltpu.make_async_remote_copy(
+        src_ref=xs.at[y],
+        dst_ref=x_far,
+        send_sem=xsend,
+        recv_sem=xrecv,
+        device_id={"feat": f ^ 4},
+        device_id_type=MESH,
+    )
+
+    def other_copy(k, src):
+        return pltpu.make_async_remote_copy(
+            src_ref=src,
+            dst_ref=x_other.at[(y + k) & (NY - 1)],
+            send_sem=osend.at[k],
+            recv_sem=orecv.at[k],
+            device_id={"feat": f ^ 1},
+            device_id_type=MESH,
+        )
+
+    far_copy.start()
+    for k in (0, 1, 3):
+        other_copy(k, xs.at[(y + k) & (NY - 1)]).start()
     add(n, remote[n].astype(jnp.float32))
 
     def take_node(k, c):
@@ -363,7 +414,10 @@
         add(source, landed[source].astype(jnp.float32))
         return c
 
-    lax.fori_loop(1, NN, take_node, 0)
+    lax.fori_loop(1, NN - 6, take_node, 0)
+    far_copy.wait_recv()
+    other_copy(2, x_far).start()
+    lax.fori_loop(NN - 6, NN, take_node, 0)
     gz[...] = acc[...].astype(jnp.bfloat16)
 
     def feat_copy(k, to, source):
@@ -381,52 +435,25 @@
         return c
 
     lax.fori_loop(1, NF, start_feat, 0)
-    gz_rows[:, pl.ds(pl.multiple_of(f * CW, CW), CW), :] = gz[pl.ds(f * GD, GD)]
-    wt = w_ref[...].astype(jnp.float32).T.astype(jnp.bfloat16)
-
-    def wait_feat(k, c):
-        feat_copy(k, feat_at(f, k), feat_back(f, k)).wait_recv()
-        return c
-
-    lax.fori_loop(1, NF, wait_feat, 0)
-
-    total = jnp.zeros((F, F), jnp.float32)
-    for h in range(GD):
-        total = total + jnp.dot(
-            gz_rows[h], x_ref[h * LO : (h + 1) * LO, :], preferred_element_type=jnp.float32
-        )
-    wpart[...] = total.reshape(NF, CW, F)
-
-    def part_copy(k, to, source):
-        return pltpu.make_async_remote_copy(
-            src_ref=wpart.at[to],
-            dst_ref=wland.at[source],
-            send_sem=wsend.at[k],
-            recv_sem=wrecv.at[k],
-            device_id={"feat": to},
-            device_id_type=MESH,
-        )
-
-    def start_part(k, c):
-        part_copy(k, feat_at(f, k), f).start()
-        return c
-
-    lax.fori_loop(1, NF, start_part, 0)
-    wland[f] = wpart[f]
-    for h in range(GD):
-        rows = gz_rows[h].astype(jnp.float32).T.astype(jnp.bfloat16)
-        in_grad[h * LO : (h + 1) * LO, :] = jnp.dot(
-            rows, wt, preferred_element_type=jnp.float32
-        ).astype(jnp.bfloat16)
-
-    def wait_part(k, c):
-        part_copy(k, feat_at(f, k), feat_back(f, k)).wait_recv()
-        return c
-
-    lax.fori_loop(1, NF, wait_part, 0)
-    mine = wland[0]
-    for g in range(1, NF):
-        mine = mine + wland[g]
+    for k in range(NY):
+        other_copy(k, x_far).wait_recv()
+
+    def product(rows, at, group):
+        out = jnp.zeros((CW, F), jnp.float32)
+        for j in range(GD):
+            out = out + jnp.dot(
+                gz[group + j],
+                rows[at, j * LO : (j + 1) * LO, :],
+                preferred_element_type=jnp.float32,
+            )
+        return out
+
+    mine = product(x_far.reshape(1, RD, F), 0, GD * (2 * far + core))
+    for k in (0, 1, 3):
+        at = (y + k) & (NY - 1)
+        mine = mine + product(xs, at, GD * (2 * at + core))
+    for at in range(NY):
+        mine = mine + product(x_other, at, GD * (2 * at + 1 - core))
     mine = mine * (1.0 / math.sqrt(NN * ROWB * BLK))
     z, x = n & -XS, n & (XS - 1)
     pieces[...] = mine.reshape(XS, CW // XS, F)
@@ -467,6 +494,21 @@
 
     for k in range(1, ZS):
         z_copy(k, n).start()
+
+    gz_rows[:, pl.ds(pl.multiple_of(f * CW, CW), CW), :] = gz[pl.ds(f * GD, GD)]
+    wt = w_ref[...].astype(jnp.float32).T.astype(jnp.bfloat16)
+
+    def wait_feat(k, c):
+        feat_copy(k, feat_at(f, k), feat_back(f, k)).wait_recv()
+        return c
+
+    lax.fori_loop(1, NF, wait_feat, 0)
+    for h in range(GD):
+        rows = gz_rows[h].astype(jnp.float32).T.astype(jnp.bfloat16)
+        in_grad[h * LO : (h + 1) * LO, :] = jnp.dot(
+            rows, wt, preferred_element_type=jnp.float32
+        ).astype(jnp.bfloat16)
+
     zland[lax.shift_right_logical(n, 2)] = zpart[...]
     for k in range(1, ZS):
         z_copy(k, z_at(ZS - k)).wait_recv()
@@ -504,13 +546,15 @@
 
     def finish_feat(k, c):
         feat_copy(k, feat_at(f, k), f).wait_send()
-        part_copy(k, feat_at(f, k), f).wait_send()
         return c
 
     lax.fori_loop(1, NF, finish_feat, 0)
-
-
-def backward(remote, local, lists, features, weight):
+    far_copy.wait_send()
+    for k in range(NY):
+        other_copy(k, x_far).wait_send()
+
+
+def backward(remote, local, lists, xs, weight):
     dma = pltpu.SemaphoreType.DMA
     return pl.pallas_call(
         backward_kernel,
@@ -518,15 +562,21 @@
             jax.ShapeDtypeStruct((RD, F), jnp.bfloat16),
             jax.ShapeDtypeStruct((CW, F), jnp.float32),
         ),
-        in_specs=[pl.BlockSpec(memory_space=VMEM)] * 5,
+        in_specs=[
+            pl.BlockSpec(memory_space=VMEM),
+            pl.BlockSpec(memory_space=VMEM),
+            pl.BlockSpec(memory_space=VMEM),
+            pl.BlockSpec(memory_space=VMEM),
+            pl.BlockSpec(memory_space=VMEM),
+        ],
         out_specs=(pl.BlockSpec(memory_space=VMEM),) * 2,
         scratch_shapes=[
+            VMEM((RD, F), jnp.bfloat16),
+            VMEM((NY, RD, F), jnp.bfloat16),
             VMEM((NN, CW, HP), jnp.bfloat16),
             VMEM((GP, CW, LO), jnp.float32),
             VMEM((GP, CW, LO), jnp.bfloat16),
             VMEM((GD, F, LO), jnp.bfloat16),
-            VMEM((NF, CW, F), jnp.float32),
-            VMEM((NF, CW, F), jnp.float32),
             VMEM((XS, CW // XS, F), jnp.float32),
             VMEM((XS, CW // XS, F), jnp.float32),
             VMEM((CW // XS, F), jnp.float32),
@@ -536,8 +586,10 @@
             dma((NN,)),
             dma((NF,)),
             dma((NF,)),
-            dma((NF,)),
-            dma((NF,)),
+            dma,
+            dma,
+            dma((NY,)),
+            dma((NY,)),
             dma((XS,)),
             dma((XS,)),
             dma((ZS,)),
@@ -549,15 +601,15 @@
             collective_id=1, has_side_effects=True, vmem_limit_bytes=32 * 2**20
         ),
         name="return_and_sum",
-    )(remote, local, lists, features, weight)
+    )(remote, local, lists, xs, weight)
 
 
 def body(features, weight, adjacency, block_coords, block_counts, send_rows, cotangent):
-    own, halo, held, cot, coords = forward(
+    own, halo, xs, held, cot, coords = forward(
         features, weight, send_rows, adjacency, cotangent, block_coords
     )
     activations, local, remote = blocks(coords, block_counts, held, own, halo, cot)
-    input_grad, weight_grad_t = backward(remote, local, send_rows, features, weight)
+    input_grad, weight_grad_t = backward(remote, local, send_rows, xs, weight)
     weight_grad = weight_grad_t.T
     return (activations, input_grad, weight_grad)
 

time: 105 us -> 94.2 us (0.90)
  Pallas kernels: 101 us -> 91.1 us
    pallas_call x1, Pallas kernels: 49.4 us -> 39 us  [backward(): pl.pallas_call(backward_kernel, out_shape=(jax.ShapeDtypeStruct((RD, F),...]
where the time goes in v3:
time: 94.2 us; the launch traced here: 93.8 us
  Pallas kernels  91.1 us (97%)
  local copies, waits for them, and re-layouts  1.42 us (2%)
  between operations  1.33 us (1%)
    pallas_call x1, Pallas kernels, backward(): pl.pallas_call(backward_kernel, out_shape=(jax.ShapeDtypeStruct((RD, F),...  39 us
    pallas_call x1, Pallas kernels, forward(): pl.pallas_call(forward_kernel, out_shape=(part, part, jax.ShapeDtypeStruc...  36.6 us
    pallas_call x1, Pallas kernels, blocks(): pl.pallas_call(blocks_kernel, out_shape=(jax.ShapeDtypeStruct((CW, ROWB *...  15.4 us

profile of v3, /device:TPU:32, one launch (start us, length us, event | category | flops | bytes accessed | tf_op | source)
XLA Modules:
  0.0 93.8 jit_solution(11808267721821278938)
XLA Ops:
  1.3 0.0 copy-start
  1.3 0.0 copy-start.1
  1.3 36.6 %project_and_send.1 = (bf16[32,32,256]{2,1,0:T(8,128)(2,1)S(1)}, bf16[32,32,256]{2,1,0:T(8,128)(2,1)S(1)}, bf16[4,1024,256]{2,1,0:T(8,128)(2,1)S(1)}, bf16[512,1...) custom-call(bf16[1024,256]{1,0:T(8,128)(2,1)} %x_hbm.1, bf16[256,256]{1,0:T(8,128)(2,1)} %w_ref.1, ...), custom_call_target="tpu_custom_call" | custom-call | tf_op jit(solution)/shard_map/project_and_send/pallas_call | solution.py:204
  37.9 15.4 %blocks.1 = (bf16[32,8192]{1,0:T(8,128)(2,1)}, f32[32,32,256]{2,1,0:T(8,128)S(1)}, bf16[32,32,256]{2,1,0:T(8,128)(2,1)S(1)}) custom-call(s32[2,512]{1,0:T(2,128)S(1)} %get-tuple-element.14.coords_v, s32[1]{0:T(128)S(6)} %copy.12.counts, bf16[512,128,128]{2,1,0:T(8,128)(2,1)S(1)} %get-tuple-element.15.held, bf16[32,32,256]{2,1,0:T(8,128)(2,1)S(1)} %get-tuple-element.16.own, ...), custom_call_target="tpu_custom_call" | custom-call | tf_op jit(solution)/shard_map/blocks/pallas_call | solution.py:316
  53.4 0.0 copy-done
  53.4 0.0 copy-done.1
  53.4 39.0 %return_and_sum.1 = (bf16[1024,256]{1,0:T(8,128)(2,1)S(1)}, f32[32,256]{1,0:T(8,128)S(1)}) custom-call(bf16[32,32,256]{2,1,0:T(8,128)(2,1)S(1)} %get-tuple-element.20.remote, f32[32,32,256]{2,1,0:T(8,128)S(1)} %get-tuple-element.21.local, s32[32,256]{1,0:T(8,128)S(1)} %copy-done.1, bf16[4,1024,256]{2,1,0:T(8,128)(2,1)S(1)} %get-tuple-element.22.xs, ...), custom_call_target="tpu_custom_call" | custom-call | tf_op jit(solution)/shard_map/return_and_sum/pallas_call | solution.py:559
  92.4 0.8 copy.13
  93.2 0.6 copy.14
Async XLA Ops:
  1.3 52.1 %copy-start = (bf16[256,256]{1,0:T(8,128)(2,1)S(1)}, bf16[256,256]{1,0:T(8,128)(2,1)}, u32[]{:S(2)}) copy-start(bf16[256,256]{1,0:T(8,128)(2,1)} %w_ref.1) | copy-start | bytes 393220
  1.3 52.1 %copy-start.1 = (s32[32,256]{1,0:T(8,128)S(1)}, s32[32,256]{1,0:T(8,128)}, u32[]{:S(2)}) copy-start(s32[32,256]{1,0:T(8,128)} %lists.1) | copy-start | bytes 98308

commit v4 on v3

--- a/solution.py
+++ b/solution.py
@@ -20,6 +20,7 @@
 GP = NF * GD
 HP = 256
 BLK = 128
+NT = (((1,), (1,)), ((), ()))
 ROWB = 64
 COLB = 128
 MAXB = 512
@@ -37,6 +38,10 @@
     z = ((n & -XS) + NN - (k & -XS)) & (NN - 1)
     x = (n + XS - (k & (XS - 1))) & (XS - 1)
     return z + x
+
+
+def far_first(i):
+    return ZS // 2 + (i // 2) * (1 - (i & 1)) - ((i + 1) // 2) * (i & 1)
 
 
 def feat_at(f, k):
@@ -145,9 +150,11 @@
     for k in (1, 3):
         rows_copy(k, y).start()
 
-    def pick(p):
-        hot, hi = one_hot_t(lists, p)
-        got = jnp.zeros((CW, HP), jnp.float32)
+    def pick(lists_at):
+        hots = [one_hot_t(lists, p) for p in lists_at]
+        hot = jnp.concatenate([h for h, _ in hots], axis=1)
+        hi = jnp.concatenate([h for _, h in hots], axis=1)
+        got = jnp.zeros((CW, len(hots) * HP), jnp.float32)
         step = 8
         for g in range(0, GP, step):
             part = jnp.dot(
@@ -155,7 +162,8 @@
             )
             for h in range(step):
                 got = jnp.where(hi == g + h, part[h * CW : (h + 1) * CW], got)
-        return got.astype(jnp.bfloat16)
+        got = got.astype(jnp.bfloat16)
+        return [got[:, i * HP : (i + 1) * HP] for i in range(len(hots))]
 
     def node_copy(k, to, source):
         return pltpu.make_async_remote_copy(
@@ -167,15 +175,22 @@
             device_id_type=MESH,
         )
 
-    def send_node(i, c):
-        k = NN - i
-        to = node_at(n, k)
-        packed[k] = pick(to)
-        node_copy(k, to, n).start()
-        return c
-
-    lax.fori_loop(1, NN, send_node, 0)
-    halo[n] = pick(n)
+    def send_nodes(i, c):
+        ks = [far_first(i) * XS + j for j in range(XS)]
+        tos = [node_at(n, k) for k in ks]
+        for k, to, got in zip(ks, tos, pick(tos)):
+            packed[k] = got
+            node_copy(k, to, n).start()
+        return c
+
+    lax.fori_loop(0, ZS - 1, send_nodes, 0)
+    tos = [node_at(n, k) for k in range(XS)]
+    for k, (to, got) in enumerate(zip(tos, pick(tos))):
+        if k == 0:
+            halo[n] = got
+        else:
+            packed[k] = got
+            node_copy(k, to, n).start()
 
     def finish_node(i, c):
         k = NN - i
@@ -238,8 +253,7 @@
     )
 
 
-UNROLL = 32
-NT = (((1,), (1,)), ((), ()))
+UNROLL = 64
 
 
 def blocks_kernel(
@@ -355,16 +369,22 @@
     barrier = enter(n, f)
     acc[...] = local[...]
 
-    def add(p, vals):
-        hot, hi = one_hot_t(lists, p)
+    def add(lists_at, vals):
+        hots = [one_hot_t(lists, p) for p in lists_at]
+        hot = jnp.concatenate([h for h, _ in hots], axis=1)
         step = 8
         for g in range(0, GP, step):
             rows = jnp.concatenate(
-                [jnp.where(hi == g + h, vals, 0.0).astype(jnp.bfloat16) for h in range(step)], axis=0
+                [
+                    jnp.concatenate(
+                        [jnp.where(hi == g + h, v, 0.0).astype(jnp.bfloat16) for h in range(step)],
+                        axis=0,
+                    )
+                    for (_, hi), v in zip(hots, vals)
+                ],
+                axis=1,
             )
-            term = lax.dot_general(
-                rows, hot, (((1,), (1,)), ((), ())), preferred_element_type=jnp.float32
-            )
+            term = lax.dot_general(rows, hot, NT, preferred_element_type=jnp.float32)
             acc[g : g + step] = acc[g : g + step] + term.reshape(step, CW, LO)
 
     pl.semaphore_wait(barrier, NN + NF - 2)
@@ -379,11 +399,16 @@
             device_id_type=MESH,
         )
 
-    def start_node(k, c):
+    for k in range(1, XS):
         node_copy(k, node_at(n, k), n).start()
-        return c
-
-    lax.fori_loop(1, NN, start_node, 0)
+
+    def start_nodes(i, c):
+        for j in range(XS):
+            k = far_first(i) * XS + j
+            node_copy(k, node_at(n, k), n).start()
+        return c
+
+    lax.fori_loop(0, ZS - 1, start_nodes, 0)
     far_copy = pltpu.make_async_remote_copy(
         src_ref=xs.at[y],
         dst_ref=x_far,
@@ -406,18 +431,24 @@
     far_copy.start()
     for k in (0, 1, 3):
         other_copy(k, xs.at[(y + k) & (NY - 1)]).start()
-    add(n, remote[n].astype(jnp.float32))
-
-    def take_node(k, c):
-        source = node_back(n, k)
-        node_copy(k, node_at(n, k), source).wait_recv()
-        add(source, landed[source].astype(jnp.float32))
-        return c
-
-    lax.fori_loop(1, NN - 6, take_node, 0)
+    sources = [node_back(n, k) for k in range(XS)]
+    for k in range(1, XS):
+        node_copy(k, node_at(n, k), sources[k]).wait_recv()
+    landed[n] = remote[n]
+    add(sources, [landed[p].astype(jnp.float32) for p in sources])
+
+    def take_nodes(i, c):
+        ks = [far_first(i) * XS + j for j in range(XS)]
+        sources = [node_back(n, k) for k in ks]
+        for k, p in zip(ks, sources):
+            node_copy(k, node_at(n, k), p).wait_recv()
+        add(sources, [landed[p].astype(jnp.float32) for p in sources])
+        return c
+
+    lax.fori_loop(0, ZS - 2, take_nodes, 0)
     far_copy.wait_recv()
     other_copy(2, x_far).start()
-    lax.fori_loop(NN - 6, NN, take_node, 0)
+    take_nodes(ZS - 2, 0)
     gz[...] = acc[...].astype(jnp.bfloat16)
 
     def feat_copy(k, to, source):

time: 94.2 us -> 87.8 us (0.932)
  Pallas kernels: 91.1 us -> 84.7 us
    pallas_call x1, Pallas kernels: 36.6 us -> 34 us  [forward(): pl.pallas_call(forward_kernel, out_shape=(part, part, jax.ShapeDtypeStruc...]
    pallas_call x1, Pallas kernels: 15.4 us -> 13.2 us  [blocks(): pl.pallas_call(blocks_kernel, out_shape=(jax.ShapeDtypeStruct((CW, ROWB *...]
    pallas_call x1, Pallas kernels: 39 us -> 37.4 us  [backward(): pl.pallas_call(backward_kernel, out_shape=(jax.ShapeDtypeStruct((RD, F),...]
where the time goes in v4:
time: 87.8 us; the launch traced here: 87.4 us
  Pallas kernels  84.7 us (96%)
  local copies, waits for them, and re-layouts  1.42 us (2%)
  between operations  1.33 us (2%)
    pallas_call x1, Pallas kernels, backward(): pl.pallas_call(backward_kernel, out_shape=(jax.ShapeDtypeStruct((RD, F),...  37.4 us
    pallas_call x1, Pallas kernels, forward(): pl.pallas_call(forward_kernel, out_shape=(part, part, jax.ShapeDtypeStruc...  34 us
    pallas_call x1, Pallas kernels, blocks(): pl.pallas_call(blocks_kernel, out_shape=(jax.ShapeDtypeStruct((CW, ROWB *...  13.2 us

profile of v4, /device:TPU:32, one launch (start us, length us, event | category | flops | bytes accessed | tf_op | source)
XLA Modules:
  0.0 87.4 jit_solution(15663475919415134965)
XLA Ops:
  1.3 0.0 copy-start
  1.3 0.0 copy-start.1
  1.3 34.0 %project_and_send.1 = (bf16[32,32,256]{2,1,0:T(8,128)(2,1)S(1)}, bf16[32,32,256]{2,1,0:T(8,128)(2,1)S(1)}, bf16[4,1024,256]{2,1,0:T(8,128)(2,1)S(1)}, bf16[512,1...) custom-call(bf16[1024,256]{1,0:T(8,128)(2,1)} %x_hbm.1, bf16[256,256]{1,0:T(8,128)(2,1)} %w_ref.1, ...), custom_call_target="tpu_custom_call" | custom-call | tf_op jit(solution)/shard_map/project_and_send/pallas_call | solution.py:219
  35.4 13.2 %blocks.1 = (bf16[32,8192]{1,0:T(8,128)(2,1)}, f32[32,32,256]{2,1,0:T(8,128)S(1)}, bf16[32,32,256]{2,1,0:T(8,128)(2,1)S(1)}) custom-call(s32[2,512]{1,0:T(2,128)S(1)} %get-tuple-element.14.coords_v, s32[1]{0:T(128)S(6)} %copy.12.counts, bf16[512,128,128]{2,1,0:T(8,128)(2,1)S(1)} %get-tuple-element.15.held, bf16[32,32,256]{2,1,0:T(8,128)(2,1)S(1)} %get-tuple-element.16.own, ...), custom_call_target="tpu_custom_call" | custom-call | tf_op jit(solution)/shard_map/blocks/pallas_call | solution.py:330
  48.6 0.0 copy-done
  48.6 0.0 copy-done.1
  48.6 37.4 %return_and_sum.1 = (bf16[1024,256]{1,0:T(8,128)(2,1)S(1)}, f32[32,256]{1,0:T(8,128)S(1)}) custom-call(bf16[32,32,256]{2,1,0:T(8,128)(2,1)S(1)} %get-tuple-element.20.remote, f32[32,32,256]{2,1,0:T(8,128)S(1)} %get-tuple-element.21.local, s32[32,256]{1,0:T(8,128)S(1)} %copy-done.1, bf16[4,1024,256]{2,1,0:T(8,128)(2,1)S(1)} %get-tuple-element.22.xs, ...), custom_call_target="tpu_custom_call" | custom-call | tf_op jit(solution)/shard_map/return_and_sum/pallas_call | solution.py:590
  86.0 0.8 copy.13
  86.8 0.6 copy.14
Async XLA Ops:
  1.3 47.3 %copy-start = (bf16[256,256]{1,0:T(8,128)(2,1)S(1)}, bf16[256,256]{1,0:T(8,128)(2,1)}, u32[]{:S(2)}) copy-start(bf16[256,256]{1,0:T(8,128)(2,1)} %w_ref.1) | copy-start | bytes 393220
  1.3 47.3 %copy-start.1 = (s32[32,256]{1,0:T(8,128)S(1)}, s32[32,256]{1,0:T(8,128)}, u32[]{:S(2)}) copy-start(s32[32,256]{1,0:T(8,128)} %lists.1) | copy-start | bytes 98308

commit v5 on v4

--- a/solution.py
+++ b/solution.py
@@ -253,7 +253,8 @@
     )
 
 
-UNROLL = 64
+UNROLL = 128
+WIDE = 4
 
 
 def blocks_kernel(
@@ -276,15 +277,16 @@
     def gather(j, c):
         base = j * UNROLL
         terms = []
-        for b in [base + u for u in range(0, UNROLL, 2)]:
-            cols = jnp.concatenate([ext[coords[1, b]], ext[coords[1, b + 1]]], axis=0)
-            pair = lax.dot_general(
+        for b in [base + u for u in range(0, UNROLL, WIDE)]:
+            cols = jnp.concatenate([ext[coords[1, b + i]] for i in range(WIDE)], axis=0)
+            part = lax.dot_general(
                 cols,
-                held[pl.ds(b, 2)].reshape(2 * BLK, BLK),
+                held[pl.ds(b, WIDE)].reshape(WIDE * BLK, BLK),
                 NT,
                 preferred_element_type=jnp.float32,
             )
-            terms += [pair[:CW, :BLK], pair[CW:, BLK:]]
+            for i in range(WIDE):
+                terms.append(part[i * CW : (i + 1) * CW, i * BLK : (i + 1) * BLK])
         for u in range(UNROLL):
             r = row_of(base + u)
             pre[r] = pre[r] + terms[u]
@@ -367,7 +369,6 @@
     core = f & 1
     far = y ^ 2
     barrier = enter(n, f)
-    acc[...] = local[...]
 
     def add(lists_at, vals):
         hots = [one_hot_t(lists, p) for p in lists_at]
@@ -431,6 +432,7 @@
     far_copy.start()
     for k in (0, 1, 3):
         other_copy(k, xs.at[(y + k) & (NY - 1)]).start()
+    acc[...] = local[...]
     sources = [node_back(n, k) for k in range(XS)]
     for k in range(1, XS):
         node_copy(k, node_at(n, k), sources[k]).wait_recv()

time: 87.8 us -> 85.1 us (0.969)
  Pallas kernels: 84.7 us -> 82.2 us
    pallas_call x1, Pallas kernels: 13.2 us -> 10.5 us  [blocks(): pl.pallas_call(blocks_kernel, out_shape=(jax.ShapeDtypeStruct((CW, ROWB *...]
where the time goes in v5:
time: 85.1 us; the launch traced here: 84.9 us
  Pallas kernels  82.2 us (97%)
  local copies, waits for them, and re-layouts  1.42 us (2%)
  between operations  1.33 us (2%)
    pallas_call x1, Pallas kernels, backward(): pl.pallas_call(backward_kernel, out_shape=(jax.ShapeDtypeStruct((RD, F),...  37.7 us
    pallas_call x1, Pallas kernels, forward(): pl.pallas_call(forward_kernel, out_shape=(part, part, jax.ShapeDtypeStruc...  34 us
    pallas_call x1, Pallas kernels, blocks(): pl.pallas_call(blocks_kernel, out_shape=(jax.ShapeDtypeStruct((CW, ROWB *...  10.5 us

profile of v5, /device:TPU:32, one launch (start us, length us, event | category | flops | bytes accessed | tf_op | source)
XLA Modules:
  0.0 84.9 jit_solution(207158161946885253)
XLA Ops:
  1.3 0.0 copy-start
  1.3 0.0 copy-start.1
  1.3 34.0 %project_and_send.1 = (bf16[32,32,256]{2,1,0:T(8,128)(2,1)S(1)}, bf16[32,32,256]{2,1,0:T(8,128)(2,1)S(1)}, bf16[4,1024,256]{2,1,0:T(8,128)(2,1)S(1)}, bf16[512,1...) custom-call(bf16[1024,256]{1,0:T(8,128)(2,1)} %x_hbm.1, bf16[256,256]{1,0:T(8,128)(2,1)} %w_ref.1, ...), custom_call_target="tpu_custom_call" | custom-call | tf_op jit(solution)/shard_map/project_and_send/pallas_call | solution.py:219
  35.4 10.5 %blocks.1 = (bf16[32,8192]{1,0:T(8,128)(2,1)}, f32[32,32,256]{2,1,0:T(8,128)S(1)}, bf16[32,32,256]{2,1,0:T(8,128)(2,1)S(1)}) custom-call(s32[2,512]{1,0:T(2,128)S(1)} %get-tuple-element.14.coords_v, s32[1]{0:T(128)S(6)} %copy.12.counts, bf16[512,128,128]{2,1,0:T(8,128)(2,1)S(1)} %get-tuple-element.15.held, bf16[32,32,256]{2,1,0:T(8,128)(2,1)S(1)} %get-tuple-element.16.own, ...), custom_call_target="tpu_custom_call" | custom-call | tf_op jit(solution)/shard_map/blocks/pallas_call | solution.py:332
  45.8 0.0 copy-done
  45.8 0.0 copy-done.1
  45.9 37.7 %return_and_sum.1 = (bf16[1024,256]{1,0:T(8,128)(2,1)S(1)}, f32[32,256]{1,0:T(8,128)S(1)}) custom-call(bf16[32,32,256]{2,1,0:T(8,128)(2,1)S(1)} %get-tuple-element.20.remote, f32[32,32,256]{2,1,0:T(8,128)S(1)} %get-tuple-element.21.local, s32[32,256]{1,0:T(8,128)S(1)} %copy-done.1, bf16[4,1024,256]{2,1,0:T(8,128)(2,1)S(1)} %get-tuple-element.22.xs, ...), custom_call_target="tpu_custom_call" | custom-call | tf_op jit(solution)/shard_map/return_and_sum/pallas_call | solution.py:592
  83.5 0.8 copy.13
  84.3 0.6 copy.14
Async XLA Ops:
  1.3 44.6 %copy-start = (bf16[256,256]{1,0:T(8,128)(2,1)S(1)}, bf16[256,256]{1,0:T(8,128)(2,1)}, u32[]{:S(2)}) copy-start(bf16[256,256]{1,0:T(8,128)(2,1)} %w_ref.1) | copy-start | bytes 393220
  1.3 44.6 %copy-start.1 = (s32[32,256]{1,0:T(8,128)S(1)}, s32[32,256]{1,0:T(8,128)}, u32[]{:S(2)}) copy-start(s32[32,256]{1,0:T(8,128)} %lists.1) | copy-start | bytes 98308

commit v6 on v5

--- a/solution.py
+++ b/solution.py
@@ -175,15 +175,20 @@
             device_id_type=MESH,
         )
 
-    def send_nodes(i, c):
-        ks = [far_first(i) * XS + j for j in range(XS)]
+    def send_some(ks):
         tos = [node_at(n, k) for k in ks]
         for k, to, got in zip(ks, tos, pick(tos)):
             packed[k] = got
             node_copy(k, to, n).start()
-        return c
-
-    lax.fori_loop(0, ZS - 1, send_nodes, 0)
+
+    def send_nodes(i, c):
+        send_some([far_first(i) * XS + j for j in range(XS)])
+        return c
+
+    first = far_first(0) * XS
+    send_some([first])
+    send_some([first + j for j in range(1, XS)])
+    lax.fori_loop(1, ZS - 1, send_nodes, 0)
     tos = [node_at(n, k) for k in range(XS)]
     for k, (to, got) in enumerate(zip(tos, pick(tos))):
         if k == 0:
@@ -263,8 +268,7 @@
     load = pltpu.make_async_copy(coords_v, coords, sem)
     load.start()
     count = counts[0]
-    pre[...] = jnp.zeros_like(pre)
-    grad[...] = jnp.zeros_like(grad)
+    pre[ROWB] = jnp.zeros((CW, BLK), jnp.float32)
     for g in range(GP):
         for s in range(2):
             ext[2 * g + s] = own[g, :, s * BLK : (s + 1) * BLK]
@@ -274,7 +278,7 @@
     def row_of(b):
         return jnp.where(b < count, coords[0, b], ROWB)
 
-    def gather(j, c):
+    def gather(j, c, stored=0):
         base = j * UNROLL
         terms = []
         for b in [base + u for u in range(0, UNROLL, WIDE)]:
@@ -289,10 +293,11 @@
                 terms.append(part[i * CW : (i + 1) * CW, i * BLK : (i + 1) * BLK])
         for u in range(UNROLL):
             r = row_of(base + u)
-            pre[r] = pre[r] + terms[u]
-        return c
-
-    lax.fori_loop(0, MAXB // UNROLL, gather, 0)
+            pre[r] = terms[u] if u < stored else pre[r] + terms[u]
+        return c
+
+    gather(0, 0, ROWB)
+    lax.fori_loop(1, MAXB // UNROLL, gather, 0)
 
     for r in range(ROWB):
         v = pre[r]
@@ -304,7 +309,7 @@
         )
     gpre[ROWB] = jnp.zeros((CW, BLK), jnp.bfloat16)
 
-    def spread(j, c):
+    def spread(j, c, stored=0):
         base = j * UNROLL
         terms = []
         for b in [base + u for u in range(0, UNROLL, 2)]:
@@ -317,10 +322,11 @@
             terms += [pair[:CW, :BLK], pair[CW:, BLK:]]
         for u in range(UNROLL):
             col = coords[1, base + u]
-            grad[col] = grad[col] + terms[u]
-        return c
-
-    lax.fori_loop(0, MAXB // UNROLL, spread, 0)
+            grad[col] = terms[u] if u < stored else grad[col] + terms[u]
+        return c
+
+    spread(0, 0, COLB)
+    lax.fori_loop(1, MAXB // UNROLL, spread, 0)
     for g in range(GP):
         for s in range(2):
             at = slice(s * BLK, (s + 1) * BLK)
@@ -360,7 +366,7 @@
 
 def backward_kernel(
     remote, local, lists, xs, w_ref, in_grad, w_grad,
-    x_far, x_other, landed, acc, gz, gz_rows, pieces, pland, zpart, zland, whole,
+    wt, x_far, x_other, landed, acc, gz, gz_rows, pieces, pland, zpart, zland, whole,
     nsend, nrecv, fsend, frecv, xsend, xrecv, osend, orecv, psend, precv, zsend, zrecv, asend, arecv,
 ):
     n = lax.axis_index("node")
@@ -432,6 +438,7 @@
     far_copy.start()
     for k in (0, 1, 3):
         other_copy(k, xs.at[(y + k) & (NY - 1)]).start()
+    wt[...] = w_ref[...].astype(jnp.float32).T.astype(jnp.bfloat16)
     acc[...] = local[...]
     sources = [node_back(n, k) for k in range(XS)]
     for k in range(1, XS):
@@ -447,10 +454,10 @@
         add(sources, [landed[p].astype(jnp.float32) for p in sources])
         return c
 
-    lax.fori_loop(0, ZS - 2, take_nodes, 0)
+    lax.fori_loop(0, ZS - 4, take_nodes, 0)
     far_copy.wait_recv()
     other_copy(2, x_far).start()
-    take_nodes(ZS - 2, 0)
+    lax.fori_loop(ZS - 4, ZS - 1, take_nodes, 0)
     gz[...] = acc[...].astype(jnp.bfloat16)
 
     def feat_copy(k, to, source):
@@ -528,20 +535,6 @@
     for k in range(1, ZS):
         z_copy(k, n).start()
 
-    gz_rows[:, pl.ds(pl.multiple_of(f * CW, CW), CW), :] = gz[pl.ds(f * GD, GD)]
-    wt = w_ref[...].astype(jnp.float32).T.astype(jnp.bfloat16)
-
-    def wait_feat(k, c):
-        feat_copy(k, feat_at(f, k), feat_back(f, k)).wait_recv()
-        return c
-
-    lax.fori_loop(1, NF, wait_feat, 0)
-    for h in range(GD):
-        rows = gz_rows[h].astype(jnp.float32).T.astype(jnp.bfloat16)
-        in_grad[h * LO : (h + 1) * LO, :] = jnp.dot(
-            rows, wt, preferred_element_type=jnp.float32
-        ).astype(jnp.bfloat16)
-
     zland[lax.shift_right_logical(n, 2)] = zpart[...]
     for k in range(1, ZS):
         z_copy(k, z_at(ZS - k)).wait_recv()
@@ -562,6 +555,20 @@
 
     for k in range(1, XS):
         back_copy(k, n).start()
+
+    gz_rows[:, pl.ds(pl.multiple_of(f * CW, CW), CW), :] = gz[pl.ds(f * GD, GD)]
+
+    def wait_feat(k, c):
+        feat_copy(k, feat_at(f, k), feat_back(f, k)).wait_recv()
+        return c
+
+    lax.fori_loop(1, NF, wait_feat, 0)
+    for h in range(GD):
+        rows = gz_rows[h].astype(jnp.float32).T.astype(jnp.bfloat16)
+        in_grad[h * LO : (h + 1) * LO, :] = jnp.dot(
+            rows, wt[...], preferred_element_type=jnp.float32
+        ).astype(jnp.bfloat16)
+
     for k in range(1, XS):
         back_copy(k, x_at(XS - k)).wait_recv()
     w_grad[...] = whole[...].reshape(CW, F)
@@ -604,6 +611,7 @@
         ],
         out_specs=(pl.BlockSpec(memory_space=VMEM),) * 2,
         scratch_shapes=[
+            VMEM((F, F), jnp.bfloat16),
             VMEM((RD, F), jnp.bfloat16),
             VMEM((NY, RD, F), jnp.bfloat16),
             VMEM((NN, CW, HP), jnp.bfloat16),

time: 85.1 us -> 83.8 us (0.985)
  Pallas kernels: 82.2 us -> 81 us
    pallas_call x1, Pallas kernels: 37.7 us -> 36.7 us  [backward(): pl.pallas_call(backward_kernel, out_shape=(jax.ShapeDtypeStruct((RD, F),...]
where the time goes in v6:
time: 83.8 us; the launch traced here: 83.7 us
  Pallas kernels  81 us (97%)
  local copies, waits for them, and re-layouts  1.42 us (2%)
  between operations  1.33 us (2%)
    pallas_call x1, Pallas kernels, backward(): pl.pallas_call(backward_kernel, out_shape=(jax.ShapeDtypeStruct((RD, F),...  36.7 us
    pallas_call x1, Pallas kernels, forward(): pl.pallas_call(forward_kernel, out_shape=(part, part, jax.ShapeDtypeStruc...  33.7 us
    pallas_call x1, Pallas kernels, blocks(): pl.pallas_call(blocks_kernel, out_shape=(jax.ShapeDtypeStruct((CW, ROWB *...  10.6 us

profile of v6, /device:TPU:32, one launch (start us, length us, event | category | flops | bytes accessed | tf_op | source)
XLA Modules:
  0.0 83.7 jit_solution(17331618870349165416)
XLA Ops:
  1.3 0.0 copy-start
  1.3 0.0 copy-start.1
  1.3 33.7 %project_and_send.1 = (bf16[32,32,256]{2,1,0:T(8,128)(2,1)S(1)}, bf16[32,32,256]{2,1,0:T(8,128)(2,1)S(1)}, bf16[4,1024,256]{2,1,0:T(8,128)(2,1)S(1)}, bf16[512,1...) custom-call(bf16[1024,256]{1,0:T(8,128)(2,1)} %x_hbm.1, bf16[256,256]{1,0:T(8,128)(2,1)} %w_ref.1, ...), custom_call_target="tpu_custom_call" | custom-call | tf_op jit(solution)/shard_map/project_and_send/pallas_call | solution.py:224
  35.0 10.6 %blocks.1 = (bf16[32,8192]{1,0:T(8,128)(2,1)}, f32[32,32,256]{2,1,0:T(8,128)S(1)}, bf16[32,32,256]{2,1,0:T(8,128)(2,1)S(1)}) custom-call(s32[2,512]{1,0:T(2,128)S(1)} %get-tuple-element.14.coords_v, s32[1]{0:T(128)S(6)} %copy.12.counts, bf16[512,128,128]{2,1,0:T(8,128)(2,1)S(1)} %get-tuple-element.15.held, bf16[32,32,256]{2,1,0:T(8,128)(2,1)S(1)} %get-tuple-element.16.own, ...), custom_call_target="tpu_custom_call" | custom-call | tf_op jit(solution)/shard_map/blocks/pallas_call | solution.py:338
  45.6 0.0 copy-done
  45.6 0.0 copy-done.1
  45.6 36.7 %return_and_sum.1 = (bf16[1024,256]{1,0:T(8,128)(2,1)S(1)}, f32[32,256]{1,0:T(8,128)S(1)}) custom-call(bf16[32,32,256]{2,1,0:T(8,128)(2,1)S(1)} %get-tuple-element.20.remote, f32[32,32,256]{2,1,0:T(8,128)S(1)} %get-tuple-element.21.local, s32[32,256]{1,0:T(8,128)S(1)} %copy-done.1, bf16[4,1024,256]{2,1,0:T(8,128)(2,1)S(1)} %get-tuple-element.22.xs, ...), custom_call_target="tpu_custom_call" | custom-call | tf_op jit(solution)/shard_map/return_and_sum/pallas_call | solution.py:599
  82.3 0.8 copy.13
  83.1 0.6 copy.14
Async XLA Ops:
  1.3 44.3 %copy-start = (bf16[256,256]{1,0:T(8,128)(2,1)S(1)}, bf16[256,256]{1,0:T(8,128)(2,1)}, u32[]{:S(2)}) copy-start(bf16[256,256]{1,0:T(8,128)(2,1)} %w_ref.1) | copy-start | bytes 393220
  1.3 44.3 %copy-start.1 = (s32[32,256]{1,0:T(8,128)S(1)}, s32[32,256]{1,0:T(8,128)}, u32[]{:S(2)}) copy-start(s32[32,256]{1,0:T(8,128)} %lists.1) | copy-start | bytes 98308

commit v7 on v6

--- a/solution.py
+++ b/solution.py
@@ -55,16 +55,10 @@
 def enter(n, f):
     barrier = pltpu.get_barrier_semaphore()
 
-    def greet_node(k, c):
+    for k in range(1, NF):
+        pl.semaphore_signal(barrier, inc=1, device_id={"feat": feat_at(f, k)}, device_id_type=MESH)
+    for k in range(1, NN):
         pl.semaphore_signal(barrier, inc=1, device_id={"node": node_at(n, k)}, device_id_type=MESH)
-        return c
-
-    def greet_feat(k, c):
-        pl.semaphore_signal(barrier, inc=1, device_id={"feat": feat_at(f, k)}, device_id_type=MESH)
-        return c
-
-    lax.fori_loop(1, NF, greet_feat, 0)
-    lax.fori_loop(1, NN, greet_node, 0)
     return barrier
 
 
@@ -258,7 +252,7 @@
     )
 
 
-UNROLL = 128
+UNROLL = 256
 WIDE = 4
 
 

time: 83.8 us -> 83.4 us (level)
  no operation moved by 1% of the time
where the time goes in v7:
time: 83.4 us; the launch traced here: 83.3 us
  Pallas kernels  80.6 us (97%)
  local copies, waits for them, and re-layouts  1.42 us (2%)
  between operations  1.33 us (2%)
    pallas_call x1, Pallas kernels, backward(): pl.pallas_call(backward_kernel, out_shape=(jax.ShapeDtypeStruct((RD, F),...  36.6 us
    pallas_call x1, Pallas kernels, forward(): pl.pallas_call(forward_kernel, out_shape=(part, part, jax.ShapeDtypeStruc...  33.6 us
    pallas_call x1, Pallas kernels, blocks(): pl.pallas_call(blocks_kernel, out_shape=(jax.ShapeDtypeStruct((CW, ROWB *...  10.4 us

profile of v7, /device:TPU:32, one launch (start us, length us, event | category | flops | bytes accessed | tf_op | source)
XLA Modules:
  0.0 83.3 jit_solution(9789459087837441738)
XLA Ops:
  1.3 0.0 copy-start
  1.3 0.0 copy-start.1
  1.3 33.6 %project_and_send.1 = (bf16[32,32,256]{2,1,0:T(8,128)(2,1)S(1)}, bf16[32,32,256]{2,1,0:T(8,128)(2,1)S(1)}, bf16[4,1024,256]{2,1,0:T(8,128)(2,1)S(1)}, bf16[512,1...) custom-call(bf16[1024,256]{1,0:T(8,128)(2,1)} %x_hbm.1, bf16[256,256]{1,0:T(8,128)(2,1)} %w_ref.1, ...), custom_call_target="tpu_custom_call" | custom-call | tf_op jit(solution)/shard_map/project_and_send/pallas_call | solution.py:218
  34.9 10.4 %blocks.1 = (bf16[32,8192]{1,0:T(8,128)(2,1)}, f32[32,32,256]{2,1,0:T(8,128)S(1)}, bf16[32,32,256]{2,1,0:T(8,128)(2,1)S(1)}) custom-call(s32[2,512]{1,0:T(2,128)S(1)} %get-tuple-element.14.coords_v, s32[1]{0:T(128)S(6)} %copy.12.counts, bf16[512,128,128]{2,1,0:T(8,128)(2,1)S(1)} %get-tuple-element.15.held, bf16[32,32,256]{2,1,0:T(8,128)(2,1)S(1)} %get-tuple-element.16.own, ...), custom_call_target="tpu_custom_call" | custom-call | tf_op jit(solution)/shard_map/blocks/pallas_call | solution.py:332
  45.3 0.0 copy-done
  45.3 0.0 copy-done.1
  45.3 36.6 %return_and_sum.1 = (bf16[1024,256]{1,0:T(8,128)(2,1)S(1)}, f32[32,256]{1,0:T(8,128)S(1)}) custom-call(bf16[32,32,256]{2,1,0:T(8,128)(2,1)S(1)} %get-tuple-element.20.remote, f32[32,32,256]{2,1,0:T(8,128)S(1)} %get-tuple-element.21.local, s32[32,256]{1,0:T(8,128)S(1)} %copy-done.1, bf16[4,1024,256]{2,1,0:T(8,128)(2,1)S(1)} %get-tuple-element.22.xs, ...), custom_call_target="tpu_custom_call" | custom-call | tf_op jit(solution)/shard_map/return_and_sum/pallas_call | solution.py:593
  81.9 0.8 copy.13
  82.7 0.6 copy.14
Async XLA Ops:
  1.3 44.0 %copy-start = (bf16[256,256]{1,0:T(8,128)(2,1)S(1)}, bf16[256,256]{1,0:T(8,128)(2,1)}, u32[]{:S(2)}) copy-start(bf16[256,256]{1,0:T(8,128)(2,1)} %w_ref.1) | copy-start | bytes 393220
  1.3 44.0 %copy-start.1 = (s32[32,256]{1,0:T(8,128)S(1)}, s32[32,256]{1,0:T(8,128)}, u32[]{:S(2)}) copy-start(s32[32,256]{1,0:T(8,128)} %lists.1) | copy-start | bytes 98308

commit v8 on v7

--- a/solution.py
+++ b/solution.py
@@ -149,7 +149,7 @@
         hot = jnp.concatenate([h for h, _ in hots], axis=1)
         hi = jnp.concatenate([h for _, h in hots], axis=1)
         got = jnp.zeros((CW, len(hots) * HP), jnp.float32)
-        step = 8
+        step = 32
         for g in range(0, GP, step):
             part = jnp.dot(
                 own[g : g + step].reshape(step * CW, LO), hot, preferred_element_type=jnp.float32
@@ -373,7 +373,7 @@
     def add(lists_at, vals):
         hots = [one_hot_t(lists, p) for p in lists_at]
         hot = jnp.concatenate([h for h, _ in hots], axis=1)
-        step = 8
+        step = 16
         for g in range(0, GP, step):
             rows = jnp.concatenate(
                 [

time: 83.4 us -> 83.3 us (level)
  no operation moved by 1% of the time
where the time goes in v8:
time: 83.3 us
  Pallas kernels  80.6 us (97%)
  local copies, waits for them, and re-layouts  1.42 us (2%)
  between operations  1.33 us (2%)
    pallas_call x1, Pallas kernels, backward(): pl.pallas_call(backward_kernel, out_shape=(jax.ShapeDtypeStruct((RD, F),...  36.5 us
    pallas_call x1, Pallas kernels, forward(): pl.pallas_call(forward_kernel, out_shape=(part, part, jax.ShapeDtypeStruc...  33.7 us
    pallas_call x1, Pallas kernels, blocks(): pl.pallas_call(blocks_kernel, out_shape=(jax.ShapeDtypeStruct((CW, ROWB *...  10.4 us

profile of v8, /device:TPU:32, one launch (start us, length us, event | category | flops | bytes accessed | tf_op | source)
XLA Modules:
  0.0 83.3 jit_solution(10927835726958096327)
XLA Ops:
  1.3 0.0 copy-start
  1.3 0.0 copy-start.1
  1.3 33.7 %project_and_send.1 = (bf16[32,32,256]{2,1,0:T(8,128)(2,1)S(1)}, bf16[32,32,256]{2,1,0:T(8,128)(2,1)S(1)}, bf16[4,1024,256]{2,1,0:T(8,128)(2,1)S(1)}, bf16[512,1...) custom-call(bf16[1024,256]{1,0:T(8,128)(2,1)} %x_hbm.1, bf16[256,256]{1,0:T(8,128)(2,1)} %w_ref.1, ...), custom_call_target="tpu_custom_call" | custom-call | tf_op jit(solution)/shard_map/project_and_send/pallas_call | solution.py:218
  35.0 10.4 %blocks.1 = (bf16[32,8192]{1,0:T(8,128)(2,1)}, f32[32,32,256]{2,1,0:T(8,128)S(1)}, bf16[32,32,256]{2,1,0:T(8,128)(2,1)S(1)}) custom-call(s32[2,512]{1,0:T(2,128)S(1)} %get-tuple-element.14.coords_v, s32[1]{0:T(128)S(6)} %copy.12.counts, bf16[512,128,128]{2,1,0:T(8,128)(2,1)S(1)} %get-tuple-element.15.held, bf16[32,32,256]{2,1,0:T(8,128)(2,1)S(1)} %get-tuple-element.16.own, ...), custom_call_target="tpu_custom_call" | custom-call | tf_op jit(solution)/shard_map/blocks/pallas_call | solution.py:332
  45.4 0.0 copy-done
  45.4 0.0 copy-done.1
  45.4 36.5 %return_and_sum.1 = (bf16[1024,256]{1,0:T(8,128)(2,1)S(1)}, f32[32,256]{1,0:T(8,128)S(1)}) custom-call(bf16[32,32,256]{2,1,0:T(8,128)(2,1)S(1)} %get-tuple-element.20.remote, f32[32,32,256]{2,1,0:T(8,128)S(1)} %get-tuple-element.21.local, s32[32,256]{1,0:T(8,128)S(1)} %copy-done.1, bf16[4,1024,256]{2,1,0:T(8,128)(2,1)S(1)} %get-tuple-element.22.xs, ...), custom_call_target="tpu_custom_call" | custom-call | tf_op jit(solution)/shard_map/return_and_sum/pallas_call | solution.py:593
  81.9 0.8 copy.13
  82.7 0.6 copy.14
Async XLA Ops:
  1.3 44.1 %copy-start = (bf16[256,256]{1,0:T(8,128)(2,1)S(1)}, bf16[256,256]{1,0:T(8,128)(2,1)}, u32[]{:S(2)}) copy-start(bf16[256,256]{1,0:T(8,128)(2,1)} %w_ref.1) | copy-start | bytes 393220
  1.3 44.1 %copy-start.1 = (s32[32,256]{1,0:T(8,128)S(1)}, s32[32,256]{1,0:T(8,128)}, u32[]{:S(2)}) copy-start(s32[32,256]{1,0:T(8,128)} %lists.1) | copy-start | bytes 98308
